TPU v7x, 32 devices: a whole 2x2x4 slice. The times are simulated.
32 devices in a mesh: groups: 2 (over y), dom: 8 (over z, x), mp: 2 (over core).
Axes of the slice: x: 2, y: 2, z: 4, core: 2. Of those that a mesh axis runs over, the one named last changes fastest.
Arguments:
- node_latent: bfloat16 [1536, 512], P(('groups', 'dom')), parts along dimension 0, may hold values from -6 to 6
- edge_latent: bfloat16 [9216, 512], P(('groups', 'dom')), parts along dimension 0, may hold values from -6 to 6
- node_cot: bfloat16 [1536, 512], P(('groups', 'dom')), parts along dimension 0, may hold values from -6 to 6
- edge_cot: bfloat16 [9216, 512], P(('groups', 'dom')), parts along dimension 0, may hold values from -6 to 6
- edge_w1: bfloat16 [1536, 512], P(None, 'mp'), may hold values from -0.15625 to 0.15625
- edge_w2: bfloat16 [512, 512], P('mp'), may hold values from -0.25 to 0.25
- node_w1: bfloat16 [1024, 512], P(None, 'mp'), may hold values from -0.1875 to 0.1875
- node_w2: bfloat16 [512, 512], P('mp'), may hold values from -0.25 to 0.25
- send_rows: int32 [8, 6, 8], P('dom'), may hold values from 0 to 95
- edge_sender: int32 [4608], P('dom'), may hold values from 0 to 143, as said below
- edge_receiver: int32 [4608], P('dom'), may hold values from 0 to 95
- edge_count: int32 [8], P('dom'), may hold values from 288 to 576, as said below
Outputs:
- node_grad: bfloat16 [1536, 512], P(('groups', 'dom')), parts along dimension 0
- edge_grad: bfloat16 [9216, 512], P(('groups', 'dom')), parts along dimension 0
- edge_w1_grad: float32 [3072, 512], P(('groups', 'dom'), 'mp'), parts along dimension 0
- edge_w2_grad: float32 [1024, 512], P(('groups', 'mp'), 'dom'), parts along dimension 0
- node_w1_grad: float32 [2048, 512], P(('groups', 'dom'), 'mp'), parts along dimension 0
- node_w2_grad: float32 [1024, 512], P(('groups', 'mp'), 'dom'), parts along dimension 0
There are 2 independent parts, one for each index of `groups`. A program takes and returns all parts, laid end to end along the dimension named above; an argument that names none is the same for every part. Nothing has to cross between parts.
Inputs may be any that keep to these rules, and one draw needn't show every extreme that they name: `edge_sender`: A code below 96 names a node of the edge's own partition; a code c of 96 or more names entry (c - 96) % 8 of the list that the edge's partition's neighbour number (c - 96) // 8 keeps for it. Among the first 48 slots of each block every code of 96 or more appears once. `edge_count`: some partition has all 576 slots live.
All inputs are finite; a program needn't handle non-finite values.
Results may differ from a plain program's by a relative error of at most 0.015.
Values may be sent and summed in bfloat16 or wider, within the bound.
A program may use at most 64 MiB of HBM per device.

v0:
```python
import jax
import jax.numpy as jnp
from jax import lax
from jax.sharding import PartitionSpec as P

EPS = 1e-05


def passed_along(shard, axis, by):
    count = lax.axis_size(axis)
    return lax.ppermute(shard, axis, [(i, (i + by) % count) for i in range(count)])


def layer_norm(values):
    center = values - jnp.mean(values, axis=-1, keepdims=True)
    inverse = lax.rsqrt(jnp.mean(center * center, axis=-1, keepdims=True) + EPS)
    return (center * inverse, inverse)


def norm_back(normed, inverse, upstream):
    first = jnp.mean(upstream, axis=-1, keepdims=True)
    second = jnp.mean(upstream * normed, axis=-1, keepdims=True)
    return inverse * (upstream - first - normed * second)


def silu_slope(values):
    sigma = jax.nn.sigmoid(values)
    return sigma * (1.0 + values * (1.0 - sigma))


def contract_rows(left, right):
    return lax.dot_general(
        left, right, (((0,), (0,)), ((), ())), preferred_element_type=jnp.float32
    )


def contract_cols(left, right):
    return lax.dot_general(
        left, right, (((1,), (1,)), ((), ())), preferred_element_type=jnp.float32
    )


def offset_of(index, half):
    return (index % half + 1) * (1 if index < half else -1)


def second_layer(activation, weight):
    partial_out = jnp.dot(activation, weight, preferred_element_type=jnp.float32)
    return lax.psum(partial_out.astype(jnp.bfloat16), "mp").astype(jnp.float32)


def weight_term(inputs, upstream):
    return contract_rows(inputs, upstream)


def local(
    node_latent,
    edge_latent,
    node_cot,
    edge_cot,
    edge_w1,
    edge_w2,
    node_w1,
    node_w2,
    send_rows,
    edge_sender,
    edge_receiver,
    edge_count,
):
    node_rows = node_latent.shape[0]
    edge_rows = edge_latent.shape[0]
    width = node_latent.shape[1]
    table = send_rows[0]
    neigh_count = table.shape[0]
    slots = table.shape[1]
    half = neigh_count // 2
    codes = node_rows + neigh_count * slots
    listed = table.reshape(-1)
    outgoing = node_latent[listed].reshape(neigh_count, slots, width)
    arrived = [
        passed_along(outgoing[index], "dom", offset_of(index, half)) for index in range(neigh_count)
    ]
    incoming = jnp.stack(arrived)
    sources = jnp.concatenate([node_latent, incoming.reshape(neigh_count * slots, width)], axis=0)
    live = (jnp.arange(edge_rows, dtype=jnp.int32) < edge_count[0]).astype(jnp.float32)[:, None]
    edge_input = jnp.concatenate(
        [edge_latent, sources[edge_sender], node_latent[edge_receiver]], axis=1
    )
    edge_pre = jnp.dot(edge_input, edge_w1, preferred_element_type=jnp.float32)
    edge_act = jax.nn.silu(edge_pre).astype(jnp.bfloat16)
    edge_out = second_layer(edge_act, edge_w2)
    edge_normed, edge_inverse = layer_norm(edge_out)
    update_b = (live * edge_normed).astype(jnp.bfloat16)
    receive_pick = (
        jnp.arange(node_rows, dtype=jnp.int32)[:, None] == edge_receiver[None, :]
    ).astype(jnp.bfloat16)
    gathered = jnp.dot(receive_pick, update_b, preferred_element_type=jnp.float32).astype(
        jnp.bfloat16
    )
    node_input = jnp.concatenate([node_latent, gathered], axis=1)
    node_pre = jnp.dot(node_input, node_w1, preferred_element_type=jnp.float32)
    node_act = jax.nn.silu(node_pre).astype(jnp.bfloat16)
    node_out = second_layer(node_act, node_w2)
    node_normed, node_inverse = layer_norm(node_out)
    node_dout = norm_back(node_normed, node_inverse, node_cot.astype(jnp.float32)).astype(
        jnp.bfloat16
    )
    node_w2_term = contract_rows(node_act, node_dout)
    node_dpre = (contract_cols(node_dout, node_w2) * silu_slope(node_pre)).astype(jnp.bfloat16)
    node_w1_grad = lax.psum_scatter(
        weight_term(node_input, node_dpre), "dom", scatter_dimension=0, tiled=True
    )
    node_dinput = lax.psum(contract_cols(node_dpre, node_w1).astype(jnp.bfloat16), "mp").astype(
        jnp.float32
    )
    gathered_grad = node_dinput[:, width:].astype(jnp.bfloat16)
    edge_dup = live * (
        edge_cot.astype(jnp.float32) + gathered_grad[edge_receiver].astype(jnp.float32)
    )
    edge_dout = norm_back(edge_normed, edge_inverse, edge_dup).astype(jnp.bfloat16)
    edge_w2_term = contract_rows(edge_act, edge_dout)
    edge_dpre = (contract_cols(edge_dout, edge_w2) * silu_slope(edge_pre)).astype(jnp.bfloat16)
    edge_w1_grad = lax.psum_scatter(
        weight_term(edge_input, edge_dpre), "dom", scatter_dimension=0, tiled=True
    )
    edge_dinput = lax.psum(contract_cols(edge_dpre, edge_w1).astype(jnp.bfloat16), "mp").astype(
        jnp.float32
    )
    edge_grad = (live * (edge_cot.astype(jnp.float32) + edge_dinput[:, :width])).astype(
        jnp.bfloat16
    )
    sender_part = (live * edge_dinput[:, width : 2 * width]).astype(jnp.bfloat16)
    receiver_part = (live * edge_dinput[:, 2 * width :]).astype(jnp.bfloat16)
    code_pick = (jnp.arange(codes, dtype=jnp.int32)[:, None] == edge_sender[None, :]).astype(
        jnp.bfloat16
    )
    per_code = jnp.dot(code_pick, sender_part, preferred_element_type=jnp.float32)
    per_node = jnp.dot(receive_pick, receiver_part, preferred_element_type=jnp.float32)
    returning = per_code[node_rows:].reshape(neigh_count, slots, width)
    backs = [
        passed_along(returning[index], "dom", -offset_of(index, half))
        for index in range(neigh_count)
    ]
    returned = jnp.stack(backs)
    remote_sum = (
        jnp.zeros((node_rows, width), jnp.float32)
        .at[listed]
        .add(returned.reshape(neigh_count * slots, width))
    )
    node_grad = (
        node_cot.astype(jnp.float32)
        + node_dinput[:, :width]
        + per_code[:node_rows]
        + per_node
        + remote_sum
    )
    edge_w2_grad, node_w2_grad = (
        lax.psum_scatter(edge_w2_term, "dom", scatter_dimension=1, tiled=True),
        lax.psum_scatter(node_w2_term, "dom", scatter_dimension=1, tiled=True),
    )
    return (
        node_grad.astype(jnp.bfloat16),
        edge_grad,
        edge_w1_grad,
        edge_w2_grad,
        node_w1_grad,
        node_w2_grad,
    )


def solution(mesh):
    placed = (
        P(("groups", "dom"), None),
        P(("groups", "dom"), None),
        P(("groups", "dom"), None),
        P(("groups", "dom"), None),
        P(None, "mp"),
        P("mp", None),
        P(None, "mp"),
        P("mp", None),
        P("dom", None, None),
        P("dom"),
        P("dom"),
        P("dom"),
    )
    return jax.shard_map(
        local,
        mesh=mesh,
        in_specs=placed,
        out_specs=(
            P(("groups", "dom"), None),
            P(("groups", "dom"), None),
            P(("groups", "dom"), "mp"),
            P(("groups", "mp"), "dom"),
            P(("groups", "dom"), "mp"),
            P(("groups", "mp"), "dom"),
        ),
        check_vma=False,
    )
```

profile of v0, /device:TPU:0, one launch (start us, length us, event | category | flops | bytes accessed | tf_op | source)
XLA Modules:
  0.0 409.2 jit_solution(3938382634406215293)
XLA Ops:
  8.7 1.6 gather_fusion
  10.3 5.0 %collective-permute-start.5 = (bf16[8,512]{1,0:T(8,128)(2,1)S(1)}, bf16[8,512]{1,0:T(8,128)(2,1)S(1)}, u32[]{:S(2)}, u32[]{:S(2)}) collective-permute-start(bf16[8,512]{1,0:T(8,128)(2,1)S(1)} %get-tuple-element.16), channel_id=1, source_target_pairs={{0,10},{2,12},{4,14},{6,0},{8,2},{10,4},{12,6},{14,8},{1,11},{3,13... | collective-permute-start | bytes 24584 | tf_op jit(solution)/shard_map/ppermute | solution.py:11
  15.3 1.3 collective-permute-start.4
  17.2 1.6 collective-permute-start.2
  18.8 2.4 collective-permute-start
  22.6 1.9 constant_dynamic-update-slice_fusion.8
  24.6 2.7 gather_fusion.2
  27.4 5.4 %collective-permute-done.1 = bf16[8,512]{1,0:T(8,128)(2,1)S(1)} collective-permute-done((bf16[8,512]{1,0:T(8,128)(2,1)S(1)}, bf16[8,512]{1,0:T(8,128)(2,1)S(1)}, u32[]{:S(2)}, u32[]{:S(2)}) %collective-permute-start.1) | collective-permute-done | bytes 8224 | tf_op jit(solution)/shard_map/ppermute | solution.py:11
  32.9 2.7 gather_fusion.1
  35.7 0.9 constant_dynamic-update-slice_fusion.7
  36.6 0.9 constant_dynamic-update-slice_fusion.6
  37.5 2.1 fusion.54
  39.7 1.2 convolution_convert_fusion.1
  41.6 15.6 %all-reduce.5.cloned.1.call-done = bf16[576,512]{1,0:T(8,128)(2,1)} async-done(((bf16[576,512]{1,0:T(8,128)(2,1)}), bf16[576,512]{1,0:T(8,128)(2,1)}) %all-reduce.5.cloned.1.call-update) | async-done | bytes 589840 | tf_op jit(solution)/shard_map/psum | solution.py:49
  57.2 1.3 convert_reduce_fusion
  58.5 1.4 fusion.11
  60.8 0.8 convolution_convert_fusion.4
  61.7 19.1 %all-reduce.7.cloned.1.call-done = bf16[96,512]{1,0:T(8,128)(2,1)} async-done(((bf16[96,512]{1,0:T(8,128)(2,1)}), bf16[96,512]{1,0:T(8,128)(2,1)}) %all-reduce.7.cloned.1.call-update) | async-done | bytes 98320 | tf_op jit(solution)/shard_map/psum | solution.py:49
  80.8 1.0 convert_reduce_fusion.2
  81.9 1.1 fusion.34
  83.0 1.1 convert_reduce_fusion.1
  84.2 1.1 fusion.17
  85.3 1.0 convolution_convert_fusion.2
  86.4 19.3 %all-reduce.9.cloned.1.call-done = bf16[96,1024]{1,0:T(8,128)(2,1)} async-done(((bf16[96,1024]{1,0:T(8,128)(2,1)}), bf16[96,1024]{1,0:T(8,128)(2,1)}) %all-reduce.9.cloned.1.call-update) | async-done | bytes 196624 | tf_op jit(solution)/shard_map/psum | solution.py:113
  105.7 0.9 slice-done
  106.6 2.7 gather_fusion.3
  111.6 1.9 convolution_convert_fusion
  113.6 0.8 copy-done.6
  114.4 1.2 fusion.48
  115.7 1.4 fusion.51
  117.2 1.3 fusion.38
  118.6 3.5 fusion.55
  122.1 13.5 %all-reduce.11.cloned.1.call-done = bf16[576,1536]{1,0:T(8,128)(2,1)} async-done(((bf16[576,1536]{1,0:T(8,128)(2,1)}), bf16[576,1536]{1,0:T(8,128)(2,1)}) %all-reduce.11.cloned.1.call-update) | async-done | bytes 1769488 | tf_op jit(solution)/shard_map/psum | solution.py:126
  135.5 1.9 convert_element_type.97
  137.9 2.7 collective-permute-start.11
  140.6 1.5 collective-permute-start.10
  142.1 1.5 collective-permute-start.9
  143.5 2.3 collective-permute-start.8
  145.9 0.9 collective-permute-start.6
  146.8 1.0 fusion.14
  148.1 1.5 collective-permute-done.6
  149.6 1.4 collective-permute-start.7
  151.0 2.3 collective-permute-done.7
  153.5 1.1 scatter_custom_fusion
  155.2 47.2 %reduce-scatter.11.cloned.1.call-done = f32[256,64]{0,1:T(8,128)} async-done(((f32[256,512]{0,1:T(8,128)}), f32[256,64]{0,1:T(8,128)}) %reduce-scatter.11.cloned.1.call-update) | async-done | bytes 65552 | tf_op jit(solution)/shard_map/reduce_scatter | solution.py:159
  202.4 65.1 %reduce-scatter.7.cloned.1.call-done = f32[256,64]{0,1:T(8,128)} async-done(((f32[256,512]{0,1:T(8,128)}), f32[256,64]{0,1:T(8,128)}) %reduce-scatter.7.cloned.1.call-update) | async-done | bytes 65552 | tf_op jit(solution)/shard_map/reduce_scatter | solution.py:158
  267.5 66.6 %reduce-scatter.9.cloned.1.call-done = f32[128,256]{1,0:T(8,128)} async-done(((f32[1024,256]{1,0:T(8,128)}), f32[128,256]{1,0:T(8,128)}) %reduce-scatter.9.cloned.1.call-update) | async-done | bytes 131088 | tf_op jit(solution)/shard_map/reduce_scatter | solution.py:110
  334.1 68.2 %reduce-scatter.5.cloned.1.call-done = f32[192,256]{1,0:T(8,128)} async-done(((f32[1536,256]{1,0:T(8,128)}), f32[192,256]{1,0:T(8,128)}) %reduce-scatter.5.cloned.1.call-update) | async-done | bytes 196624 | tf_op jit(solution)/shard_map/reduce_scatter | solution.py:123
  (124 shorter events, 8.5 us)
Async XLA Ops:
  7.2 30.3 %copy-start = (bf16[1536,256]{1,0:T(8,128)(2,1)S(1)}, bf16[1536,256]{1,0:T(8,128)(2,1)}, u32[]{:S(2)}) copy-start(bf16[1536,256]{1,0:T(8,128)(2,1)} %param.16) | copy-start | bytes 2359300
  7.2 17.4 %copy-start.1 = (bf16[96,512]{1,0:T(8,128)(2,1)S(1)}, bf16[96,512]{1,0:T(8,128)(2,1)}, u32[]{:S(2)}) copy-start(bf16[96,512]{1,0:T(8,128)(2,1)} %param.12) | copy-start | bytes 294916
  7.2 50.0 %all-reduce.5.cloned.1.call-start = ((), (), s32[]{:S(2)}) async-start(), calls=%async_computation.4 | async-start | bytes 1179648 | tf_op jit(solution)/shard_map/psum | solution.py:49
  10.3 22.6 %collective-permute-start.5 = (bf16[8,512]{1,0:T(8,128)(2,1)S(1)}, bf16[8,512]{1,0:T(8,128)(2,1)S(1)}, u32[]{:S(2)}, u32[]{:S(2)}) collective-permute-start(bf16[8,512]{1,0:T(8,128)(2,1)S(1)} %get-tuple-element.16), channel_id=1, source_target_pairs={{0,10},{2,12},{4,14},{6,0},{8,2},{10,4},{12,6},{14,8},{1,11},{3,13... | collective-permute-start | bytes 24584 | tf_op jit(solution)/shard_map/ppermute | solution.py:11
  15.3 17.6 %collective-permute-start.4 = (bf16[8,512]{1,0:T(8,128)(2,1)S(1)}, bf16[8,512]{1,0:T(8,128)(2,1)S(1)}, u32[]{:S(2)}, u32[]{:S(2)}) collective-permute-start(bf16[8,512]{1,0:T(8,128)(2,1)S(1)} %get-tuple-element.17), channel_id=1, source_target_pairs={{0,12},{2,14},{4,0},{6,2},{8,4},{10,6},{12,8},{14,10},{1,13},{3,15... | collective-permute-start | bytes 24584 | tf_op jit(solution)/shard_map/ppermute | solution.py:11
  16.6 16.2 %collective-permute-start.3 = (bf16[8,512]{1,0:T(8,128)(2,1)S(1)}, bf16[8,512]{1,0:T(8,128)(2,1)S(1)}, u32[]{:S(2)}, u32[]{:S(2)}) collective-permute-start(bf16[8,512]{1,0:T(8,128)(2,1)S(1)} %get-tuple-element.18), channel_id=1, source_target_pairs={{0,14},{2,0},{4,2},{6,4},{8,6},{10,8},{12,10},{14,12},{1,15},{3,1}... | collective-permute-start | bytes 24584 | tf_op jit(solution)/shard_map/ppermute | solution.py:11
  17.2 15.7 %collective-permute-start.2 = (bf16[8,512]{1,0:T(8,128)(2,1)S(1)}, bf16[8,512]{1,0:T(8,128)(2,1)S(1)}, u32[]{:S(2)}, u32[]{:S(2)}) collective-permute-start(bf16[8,512]{1,0:T(8,128)(2,1)S(1)} %get-tuple-element.19), channel_id=1, source_target_pairs={{0,6},{2,8},{4,10},{6,12},{8,14},{10,0},{12,2},{14,4},{1,7},{3,9},... | collective-permute-start | bytes 24584 | tf_op jit(solution)/shard_map/ppermute | solution.py:11
  18.8 8.5 %collective-permute-start = (bf16[8,512]{1,0:T(8,128)(2,1)S(1)}, bf16[8,512]{1,0:T(8,128)(2,1)S(1)}, u32[]{:S(2)}, u32[]{:S(2)}) collective-permute-start(bf16[8,512]{1,0:T(8,128)(2,1)S(1)} %get-tuple-element.21), channel_id=1, source_target_pairs={{0,2},{2,4},{4,6},{6,8},{8,10},{10,12},{12,14},{14,0},{1,3},{3,5},... | collective-permute-start | bytes 24584 | tf_op jit(solution)/shard_map/ppermute | solution.py:11
  27.3 5.5 %collective-permute-start.1 = (bf16[8,512]{1,0:T(8,128)(2,1)S(1)}, bf16[8,512]{1,0:T(8,128)(2,1)S(1)}, u32[]{:S(2)}, u32[]{:S(2)}) collective-permute-start(bf16[8,512]{1,0:T(8,128)(2,1)S(1)} %get-tuple-element.20), channel_id=1, source_target_pairs={{0,4},{2,6},{4,8},{6,10},{8,12},{10,14},{12,0},{14,2},{1,5},{3,7},... | collective-permute-start | bytes 24584 | tf_op jit(solution)/shard_map/ppermute | solution.py:11
  37.5 2.2 copy-start.20
  39.7 1.2 copy-start.26
  40.8 19.1 %copy-start.13 = (s32[576]{0:T(1024)S(1)}, s32[576]{0:T(1024)}, u32[]{:S(2)}) copy-start(s32[576]{0:T(1024)} %param.22) | copy-start | bytes 6916
  40.9 40.0 %all-reduce.7.cloned.1.call-start = ((), (), s32[]{:S(2)}) async-start(), calls=%async_computation.5 | async-start | bytes 196608 | tf_op jit(solution)/shard_map/psum | solution.py:49
  41.6 18.8 %copy-start.5 = (bf16[1024,256]{1,0:T(8,128)(2,1)S(1)}, bf16[1024,256]{1,0:T(8,128)(2,1)}, u32[]{:S(2)}) copy-start(bf16[1024,256]{1,0:T(8,128)(2,1)} %param.18) | copy-start | bytes 1572868
  57.2 2.7 copy-start.3
  59.9 1.0 copy-start.19
  60.4 22.6 %copy-start.7 = (bf16[96,512]{1,0:T(8,128)(2,1)S(1)}, bf16[96,512]{1,0:T(8,128)(2,1)}, u32[]{:S(2)}) copy-start(bf16[96,512]{1,0:T(8,128)(2,1)} %param.14) | copy-start | bytes 294916
  60.8 25.5 %copy-start.10 = (f32[96,256]{1,0:T(8,128)}, f32[96,256]{1,0:T(8,128)S(1)}, u32[]{:S(2)}) copy-start(f32[96,256]{1,0:T(8,128)S(1)} %fusion.39) | copy-start | bytes 294916
  61.7 44.0 %all-reduce.9.cloned.1.call-start = ((), (), s32[]{:S(2)}) async-start(), calls=%async_computation.6 | async-start | bytes 393216 | tf_op jit(solution)/shard_map/psum | solution.py:113
  81.9 4.5 %copy-start.14 = (f32[96]{0:T(128)}, f32[96]{0:T(128)S(1)}, u32[]{:S(2)}) copy-start(f32[96]{0:T(128)S(1)} %broadcast_multiply_fusion.5) | copy-start | bytes 1156
  83.0 3.4 copy-start.16
  84.1 2.3 copy-start.22
  84.1 2.3 copy-start.24
  85.3 1.1 copy-start.8
  86.3 49.2 %all-reduce.11.cloned.1.call-start = ((), (), s32[]{:S(2)}) async-start(), calls=%async_computation.7 | async-start | bytes 3538944 | tf_op jit(solution)/shard_map/psum | solution.py:126
  105.7 0.9 slice-start
  106.6 2.8 copy-start.4
  110.0 1.0 copy-start.21
  110.1 1.1 copy-start.27
  113.5 0.9 copy-start.11
  113.5 0.9 copy-start.15
  113.5 0.9 copy-start.17
  113.5 0.9 copy-start.23
  113.5 0.9 copy-start.25
  113.5 2.2 copy-start.28
  113.6 88.9 %reduce-scatter.11.cloned.1.call-start = ((), (), s32[]{:S(2)}) async-start(), calls=%async_computation.11 | async-start | bytes 589824 | tf_op jit(solution)/shard_map/reduce_scatter | solution.py:159
  115.7 1.5 copy-start.9
  115.7 151.8 %reduce-scatter.7.cloned.1.call-start = ((), (), s32[]{:S(2)}) async-start(), calls=%async_computation.9 | async-start | bytes 589824 | tf_op jit(solution)/shard_map/reduce_scatter | solution.py:158
  117.1 217.0 %reduce-scatter.9.cloned.1.call-start = ((), (), s32[]{:S(2)}) async-start(), calls=%async_computation.10 | async-start | bytes 1179648 | tf_op jit(solution)/shard_map/reduce_scatter | solution.py:110
  118.5 283.8 %reduce-scatter.5.cloned.1.call-start = ((), (), s32[]{:S(2)}) async-start(), calls=%async_computation.8 | async-start | bytes 1769472 | tf_op jit(solution)/shard_map/reduce_scatter | solution.py:123
  122.1 15.4 %copy-start.12 = (s32[576]{0:T(1024)S(1)}, s32[576]{0:T(1024)}, u32[]{:S(2)}) copy-start(s32[576]{0:T(1024)} %param.21) | copy-start | bytes 6916
  137.9 15.6 %collective-permute-start.11 = (f32[8,512]{1,0:T(8,128)S(1)}, f32[8,512]{1,0:T(8,128)S(1)}, u32[]{:S(2)}, u32[]{:S(2)}) collective-permute-start(f32[8,512]{1,0:T(8,128)S(1)} %get-tuple-element.10), channel_id=1, source_target_pairs={{0,6},{2,8},{4,10},{6,12},{8,14},{10,0},{12,2},{14,4},{1,7},{3,9},... | collective-permute-start | bytes 49160 | tf_op jit(solution)/shard_map/ppermute | solution.py:11
  140.6 12.9 %collective-permute-start.10 = (f32[8,512]{1,0:T(8,128)S(1)}, f32[8,512]{1,0:T(8,128)S(1)}, u32[]{:S(2)}, u32[]{:S(2)}) collective-permute-start(f32[8,512]{1,0:T(8,128)S(1)} %get-tuple-element.11), channel_id=1, source_target_pairs={{0,4},{2,6},{4,8},{6,10},{8,12},{10,14},{12,0},{14,2},{1,5},{3,7},... | collective-permute-start | bytes 49160 | tf_op jit(solution)/shard_map/ppermute | solution.py:11
  142.1 11.3 %collective-permute-start.9 = (f32[8,512]{1,0:T(8,128)S(1)}, f32[8,512]{1,0:T(8,128)S(1)}, u32[]{:S(2)}, u32[]{:S(2)}) collective-permute-start(f32[8,512]{1,0:T(8,128)S(1)} %get-tuple-element.12), channel_id=1, source_target_pairs={{0,2},{2,4},{4,6},{6,8},{8,10},{10,12},{12,14},{14,0},{1,3},{3,5},... | collective-permute-start | bytes 49160 | tf_op jit(solution)/shard_map/ppermute | solution.py:11
  143.5 9.9 %collective-permute-start.8 = (f32[8,512]{1,0:T(8,128)S(1)}, f32[8,512]{1,0:T(8,128)S(1)}, u32[]{:S(2)}, u32[]{:S(2)}) collective-permute-start(f32[8,512]{1,0:T(8,128)S(1)} %get-tuple-element.13), channel_id=1, source_target_pairs={{0,10},{2,12},{4,14},{6,0},{8,2},{10,4},{12,6},{14,8},{1,11},{3,13... | collective-permute-start | bytes 49160 | tf_op jit(solution)/shard_map/ppermute | solution.py:11
  145.9 1.9 copy-start.2
  145.9 3.7 collective-permute-start.6
  149.6 3.8 collective-permute-start.7
  (2 other events, 1.5 us)
Sparse Core Ops, SparseCore 0:
  41.0 16.1 all-reduce.4
  61.8 19.0 all-reduce.6
  86.4 19.2 all-reduce.8
  113.7 21.8 all-reduce.10
  139.3 63.0 reduce-scatter.10
  206.6 60.9 reduce-scatter.6
  271.5 62.5 reduce-scatter.8
  338.5 63.8 reduce-scatter.4
where the time goes:
time: 410 us; the launch traced here: 409 us
  waiting for transfers between devices  324 us (79%)
  starting transfers between devices  21.7 us (5%)
  matrix products  17.2 us (4%)
  local copies, waits for them, and re-layouts  16.9 us (4%)
  between operations  15.4 us (4%)
  other arithmetic  14 us (3%)
    reduce_scatter x1, waiting for transfers between devices, local(): lax.psum_scatter(weight_term(edge_input, edge_dpre), 'dom', scatter_dimen...  68.2 us
    reduce_scatter x1, waiting for transfers between devices, local(): lax.psum_scatter(weight_term(node_input, node_dpre), 'dom', scatter_dimen...  66.6 us
    reduce_scatter x1, waiting for transfers between devices, local(): lax.psum_scatter(edge_w2_term, 'dom', scatter_dimension=1, tiled=True)  65.1 us
    reduce_scatter x1, waiting for transfers between devices, local(): lax.psum_scatter(node_w2_term, 'dom', scatter_dimension=1, tiled=True)  47.2 us
    psum x2, waiting for transfers between devices, second_layer(): return lax.psum(partial_out.astype(jnp.bfloat16), 'mp').astype(jnp.float32)  34.7 us
    ppermute x12, starting transfers between devices, passed_along(): lax.ppermute(shard, axis, [(i, (i + by) % count) for i in range(count)])  21.4 us
    psum x1, waiting for transfers between devices, local(): lax.psum(contract_cols(node_dpre, node_w1).astype(jnp.bfloat16), 'mp')  19.3 us
    psum x1, waiting for transfers between devices, local(): lax.psum(contract_cols(edge_dpre, edge_w1).astype(jnp.bfloat16), 'mp')  13.5 us
  transfers between devices with their start and end apart: 20, of which 11 were waited for; matrix products, arithmetic and copies ran while one was open for 5% of the time, Pallas kernels for 0%

commit v1 on v0

v1 whole, which is shorter than its diff:
```python
import functools

import jax
import jax.numpy as jnp
from jax import lax
from jax.experimental import pallas as pl
from jax.experimental.pallas import tpu as pltpu
from jax.sharding import PartitionSpec as P

EPS = 1e-05
BF = jnp.bfloat16
F32 = jnp.float32
MESH = pl.DeviceIdType.MESH
CHUNKS = 3


def dot(left, right, contract):
    return lax.dot_general(
        left, right, (((contract[0],), (contract[1],)), ((), ())), preferred_element_type=F32
    )


def nn(left, right):
    return dot(left, right, (1, 0))


def nt(left, right):
    return dot(left, right, (1, 1))


def tn(left, right):
    return dot(left, right, (0, 0))


def layer_norm(values):
    center = values - jnp.mean(values, axis=-1, keepdims=True)
    inverse = lax.rsqrt(jnp.mean(center * center, axis=-1, keepdims=True) + EPS)
    return (center * inverse, inverse)


def norm_back(normed, inverse, upstream):
    first = jnp.mean(upstream, axis=-1, keepdims=True)
    second = jnp.mean(upstream * normed, axis=-1, keepdims=True)
    return inverse * (upstream - first - normed * second)


def silu_and_slope(values):
    sigma = jax.nn.sigmoid(values)
    return values * sigma, sigma * (1.0 + values * (1.0 - sigma))


def offset_of(index, half):
    return (index % half + 1) * (1 if index < half else -1)


def kernel(
    dims,
    node_ref,
    edge_ref,
    ncot_ref,
    ecot_ref,
    w1_ref,
    w2_ref,
    nw1_ref,
    nw2_ref,
    codes_ref,
    ngrad_ref,
    egrad_ref,
    ew1_out,
    ew2_out,
    nw1_out,
    nw2_out,
    pick,
    pick_t,
    live,
    halo_out,
    halo_in,
    sources,
    table,
    pre,
    act,
    slope,
    mine,
    theirs,
    normed,
    inverse,
    upd,
    nmine,
    ntheirs,
    gmine,
    gtheirs,
    dout,
    dpre,
    dmine,
    dtheirs,
    back_out,
    back_in,
    fmine,
    ftheirs,
    nbuf,
    np1,
    nsum,
    np2,
    ebuf,
    ep1,
    esum,
    ep2,
    halo_s,
    halo_r,
    back_s,
    back_r,
    mp_s,
    mp_r,
    n1_s,
    n1_r,
    n2_s,
    n2_r,
    e1_s,
    e1_r,
    e2_s,
    e2_r,
):
    count, neigh, slots, scatter = dims
    me = lax.axis_index("dom")
    core = lax.axis_index("mp")
    other = {"mp": 1 - core}
    nodes, width = node_ref.shape
    edges = edge_ref.shape[0]
    hidden = w2_ref.shape[0]
    listed = neigh * slots
    codes = nodes + listed
    rows = edges // CHUNKS
    half = neigh // 2

    def at(shift):
        return {"dom": lax.rem(me + shift + count, count)}

    def remote(src, dst, send, recv, device):
        return pltpu.make_async_remote_copy(
            src_ref=src,
            dst_ref=dst,
            send_sem=send,
            recv_sem=recv,
            device_id=device,
            device_id_type=MESH,
        )

    barrier = pltpu.get_barrier_semaphore()
    shifts = sorted({offset_of(k, half) % count for k in range(neigh)})
    shifts = sorted(set(shifts) | {(-s) % count for s in shifts})
    if scatter:
        shifts = list(range(1, count))
    for shift in shifts:
        pl.semaphore_signal(barrier, inc=1, device_id=at(shift), device_id_type=MESH)
    pl.semaphore_signal(barrier, inc=1, device_id=other, device_id_type=MESH)

    spread = codes_ref[...]
    place = lax.broadcasted_iota(jnp.int32, (pick.shape[0], spread.shape[1]), 0)
    hit = (place == spread[0:1, :]) | (place == spread[1:2, :])
    pick_f = jnp.where(hit, 1.0, 0.0).astype(F32)
    pick[...] = pick_f[:, :edges].astype(BF)
    send_place = lax.broadcasted_iota(jnp.int32, (nodes, listed), 0)
    lists = jnp.where(send_place == spread[2:3, :listed], 1.0, 0.0).astype(F32).astype(BF)
    node = node_ref[...]
    halo_out[...] = tn(lists, node)

    pl.semaphore_wait(barrier, len(shifts) + 1)
    halo = []
    for k in range(neigh):
        block = pl.ds(k * slots, slots)
        copy = remote(
            halo_out.at[block], halo_in.at[block], halo_s.at[k], halo_r.at[k],
            at(offset_of(k, half)),
        )
        copy.start()
        halo.append(copy)

    picked = jnp.transpose(pick_f)[:edges]
    pick_t[...] = picked.astype(BF)
    live[...] = jnp.max(picked, axis=1, keepdims=True)
    pre[...] = nn(edge_ref[...], w1_ref[0:width])
    table[0:nodes] = nn(node, w1_ref[width : 2 * width]).astype(BF)
    table[codes : codes + nodes] = nn(node, w1_ref[2 * width : 3 * width]).astype(BF)
    if pick.shape[0] > codes + nodes:
        table[codes + nodes :] = jnp.zeros((pick.shape[0] - codes - nodes, hidden), BF)
    sources[0:nodes] = node
    for copy in halo:
        copy.wait_recv()
    arrived = halo_in[...].astype(BF)
    sources[nodes:codes] = arrived
    table[nodes:codes] = nn(arrived, w1_ref[width : 2 * width]).astype(BF)

    trades = []
    for c in range(CHUNKS):
        r = pl.ds(c * rows, rows)
        values = pre[r] + nn(pick_t[r], table[...])
        a, s = silu_and_slope(values)
        a = a.astype(BF)
        act[r] = a
        slope[r] = s
        mine[r] = nn(a, w2_ref[...]).astype(BF)
        copy = remote(mine.at[r], theirs.at[r], mp_s.at[c], mp_r.at[c], other)
        copy.start()
        trades.append(copy)
    node_first = nn(node, nw1_ref[0:width])
    for c in range(CHUNKS):
        r = pl.ds(c * rows, rows)
        trades[c].wait_recv()
        n, i = layer_norm(mine[r].astype(F32) + theirs[r].astype(F32))
        normed[r] = n
        inverse[r] = i
        upd[r] = n.astype(BF)
    gathered = nn(pick[codes : codes + nodes], upd[...]).astype(BF)

    node_act, node_slope = silu_and_slope(node_first + nn(gathered, nw1_ref[width : 2 * width]))
    node_act = node_act.astype(BF)
    nmine[...] = nn(node_act, nw2_ref[...]).astype(BF)
    trade = remote(nmine, ntheirs, mp_s.at[CHUNKS], mp_r.at[CHUNKS], other)
    trade.start()
    trades.append(trade)
    trade.wait_recv()
    n, i = layer_norm(nmine[...].astype(F32) + ntheirs[...].astype(F32))
    node_dout = norm_back(n, i, ncot_ref[...].astype(F32)).astype(BF)
    node_dpre = (nt(node_dout, nw2_ref[...]) * node_slope).astype(BF)
    gmine[...] = nt(node_dpre, nw1_ref[width : 2 * width]).astype(BF)
    trade = remote(gmine, gtheirs, mp_s.at[CHUNKS + 1], mp_r.at[CHUNKS + 1], other)
    trade.start()
    trades.append(trade)

    pairs = count // 2
    x = lax.rem(me, 2)
    z = lax.div(me, 2)
    order = list(range(1, pairs)) + [0]

    def turn(k):
        return lax.rem(z + k, pairs)

    def place_slices(buf, first, second):
        a = first.shape[0] // count
        b = second.shape[0] // count
        for j in range(count):
            buf[j % 2, j // 2, 0:a] = first[j * a : (j + 1) * a].astype(BF)
            buf[j % 2, j // 2, a : a + b] = second[j * b : (j + 1) * b].astype(BF)

    def first_phase(buf, land, send, recv):
        copies = {}
        for k in order:
            copies[k] = remote(
                buf.at[1 - x, turn(k)], land.at[turn(k)], send.at[k], recv.at[k],
                {"dom": me + 1 - 2 * x},
            )
            copies[k].start()
        return copies

    def second_phase(copies, buf, land, summed, land2, send, recv):
        later = []
        for k in range(1, pairs):
            copies[k].wait_recv()
            total = buf[x, turn(k)].astype(F32) + land[turn(k)].astype(F32)
            summed[k - 1] = total.astype(BF)
            copy = remote(
                summed.at[k - 1], land2.at[k - 1], send.at[k - 1], recv.at[k - 1],
                {"dom": turn(k) * 2 + x},
            )
            copy.start()
            later.append(copy)
        return later

    def finish(copies, later, buf, land, land2, out_a, out_b):
        copies[0].wait_recv()
        total = buf[x, z].astype(F32) + land[z].astype(F32)
        for k in range(1, pairs):
            later[k - 1].wait_recv()
            total = total + land2[k - 1].astype(F32)
        a = out_a.shape[0]
        out_a[...] = total[:a]
        out_b[...] = total[a:]

    node_w1_grad = jnp.concatenate([tn(node, node_dpre), tn(gathered, node_dpre)], axis=0)
    node_w2_grad = tn(node_dout, node_act)
    if scatter:
        place_slices(nbuf, node_w1_grad, node_w2_grad)
        n_first = first_phase(nbuf, np1, n1_s, n1_r)
    else:
        nw1_out[...] = node_w1_grad
        nw2_out[...] = node_w2_grad
    node_own = nt(node_dpre, nw1_ref[0:width])

    trade.wait_recv()
    gathered_grad = (gmine[...].astype(F32) + gtheirs[...].astype(F32)).astype(BF)
    for c in range(CHUNKS):
        r = pl.ds(c * rows, rows)
        upstream = live[r] * ecot_ref[r].astype(F32) + nn(
            pick_t[r, codes : codes + nodes], gathered_grad
        )
        d = norm_back(normed[r], inverse[r], upstream).astype(BF)
        dout[r] = d
        dpre[r] = (nt(d, w2_ref[...]) * slope[r]).astype(BF)
    if scatter:
        n_later = second_phase(n_first, nbuf, np1, nsum, np2, n2_s, n2_r)
    sums = nn(pick[...], dpre[...]).astype(BF)
    by_code = sums[0:codes]
    by_node = sums[codes : codes + nodes]
    edge_w1_grad = jnp.concatenate(
        [tn(edge_ref[...], dpre[...]), tn(sources[...], by_code), tn(node, by_node)], axis=0
    )
    edge_w2_grad = tn(dout[...], act[...])
    if scatter:
        place_slices(ebuf, edge_w1_grad, edge_w2_grad)
        e_first = first_phase(ebuf, ep1, e1_s, e1_r)
    else:
        ew1_out[...] = edge_w1_grad
        ew2_out[...] = edge_w2_grad

    per_code = nt(by_code, w1_ref[width : 2 * width])
    back_out[...] = per_code[nodes:codes]
    backs = []
    for k in range(neigh):
        block = pl.ds(k * slots, slots)
        copy = remote(
            back_out.at[block], back_in.at[block], back_s.at[k], back_r.at[k],
            at(-offset_of(k, half)),
        )
        copy.start()
        backs.append(copy)
    edge_trades = []
    for c in range(CHUNKS):
        r = pl.ds(c * rows, rows)
        dmine[r] = nt(dpre[r], w1_ref[0:width]).astype(BF)
        s = CHUNKS + 2 + c
        copy = remote(dmine.at[r], dtheirs.at[r], mp_s.at[s], mp_r.at[s], other)
        copy.start()
        edge_trades.append(copy)
    node_own = node_own + per_code[0:nodes] + nt(by_node, w1_ref[2 * width : 3 * width])
    if scatter:
        e_later = second_phase(e_first, ebuf, ep1, esum, ep2, e2_s, e2_r)
    for copy in backs:
        copy.wait_recv()
    fmine[...] = node_own + nn(lists, back_in[...].astype(BF))
    last = 2 * CHUNKS + 2
    final = remote(fmine, ftheirs, mp_s.at[last], mp_r.at[last], other)
    final.start()
    for c in range(CHUNKS):
        r = pl.ds(c * rows, rows)
        edge_trades[c].wait_recv()
        total = dmine[r].astype(F32) + dtheirs[r].astype(F32)
        egrad_ref[r] = (live[r] * (ecot_ref[r].astype(F32) + total)).astype(BF)
    final.wait_recv()
    ngrad_ref[...] = (ncot_ref[...].astype(F32) + fmine[...] + ftheirs[...]).astype(BF)
    if scatter:
        finish(n_first, n_later, nbuf, np1, np2, nw1_out, nw2_out)
        finish(e_first, e_later, ebuf, ep1, ep2, ew1_out, ew2_out)
        for copy in list(n_first.values()) + n_later + list(e_first.values()) + e_later:
            copy.wait_send()
    for copy in halo + trades + backs + edge_trades + [final]:
        copy.wait_send()


def local(
    count,
    node_latent,
    edge_latent,
    node_cot,
    edge_cot,
    edge_w1,
    edge_w2,
    node_w1,
    node_w2,
    send_rows,
    edge_sender,
    edge_receiver,
    edge_count,
):
    nodes, width = node_latent.shape
    edges = edge_latent.shape[0]
    hidden = edge_w1.shape[1]
    neigh, slots = send_rows.shape[1:]
    listed = neigh * slots
    codes = nodes + listed
    total = -(-(codes + nodes) // 128) * 128
    padded = -(-edges // 128) * 128
    live = jnp.arange(edges, dtype=jnp.int32) < edge_count[0]
    fill = padded - edges
    spread = jnp.stack(
        [
            jnp.pad(jnp.where(live, edge_sender, -1), (0, fill), constant_values=-1),
            jnp.pad(jnp.where(live, edge_receiver + codes, -1), (0, fill), constant_values=-1),
            jnp.pad(send_rows.reshape(-1), (0, padded - listed), constant_values=-1),
        ]
    )
    spread = jnp.pad(spread, ((0, 5), (0, 0)), constant_values=-1)
    w1_rows, nw1_rows = edge_w1.shape[0], node_w1.shape[0]
    scatter = (
        count % 2 == 0
        and w1_rows % (16 * count) == 0
        and nw1_rows % (16 * count) == 0
        and width % (16 * count) == 0
    )
    parts = count if scatter else 1
    pairs = max(count // 2, 2) if scatter else 2
    n_rows = (nw1_rows + width) // parts if scatter else 16
    e_rows = (w1_rows + width) // parts if scatter else 16
    vmem = pltpu.VMEM
    dma = pltpu.SemaphoreType.DMA
    scratch = [
        vmem((total, edges), BF),
        vmem((edges, total), BF),
        vmem((edges, 1), F32),
        vmem((listed, width), F32),
        vmem((listed, width), F32),
        vmem((codes, width), BF),
        vmem((total, hidden), BF),
        vmem((edges, hidden), F32),
        vmem((edges, hidden), BF),
        vmem((edges, hidden), F32),
        vmem((edges, width), BF),
        vmem((edges, width), BF),
        vmem((edges, width), F32),
        vmem((edges, 1), F32),
        vmem((edges, width), BF),
        vmem((nodes, width), BF),
        vmem((nodes, width), BF),
        vmem((nodes, width), BF),
        vmem((nodes, width), BF),
        vmem((edges, width), BF),
        vmem((edges, hidden), BF),
        vmem((edges, width), BF),
        vmem((edges, width), BF),
        vmem((listed, width), F32),
        vmem((listed, width), F32),
        vmem((nodes, width), F32),
        vmem((nodes, width), F32),
        vmem((2, pairs, n_rows, hidden), BF),
        vmem((pairs, n_rows, hidden), BF),
        vmem((pairs - 1, n_rows, hidden), BF),
        vmem((pairs - 1, n_rows, hidden), BF),
        vmem((2, pairs, e_rows, hidden), BF),
        vmem((pairs, e_rows, hidden), BF),
        vmem((pairs - 1, e_rows, hidden), BF),
        vmem((pairs - 1, e_rows, hidden), BF),
        dma((neigh,)),
        dma((neigh,)),
        dma((neigh,)),
        dma((neigh,)),
        dma((2 * CHUNKS + 3,)),
        dma((2 * CHUNKS + 3,)),
        dma((pairs,)),
        dma((pairs,)),
        dma((pairs - 1,)),
        dma((pairs - 1,)),
        dma((pairs,)),
        dma((pairs,)),
        dma((pairs - 1,)),
        dma((pairs - 1,)),
    ]
    shape = jax.ShapeDtypeStruct
    node_grad, edge_grad, ew1, ew2, nw1, nw2 = pl.pallas_call(
        functools.partial(kernel, (count, neigh, slots, scatter)),
        out_shape=(
            shape((nodes, width), BF),
            shape((edges, width), BF),
            shape((w1_rows // parts, hidden), F32),
            shape((width // parts, hidden), F32),
            shape((nw1_rows // parts, hidden), F32),
            shape((width // parts, hidden), F32),
        ),
        in_specs=[pl.BlockSpec(memory_space=pltpu.VMEM)] * 9,
        out_specs=[pl.BlockSpec(memory_space=pltpu.VMEM)] * 6,
        scratch_shapes=scratch,
        compiler_params=pltpu.CompilerParams(
            collective_id=0, has_side_effects=True, vmem_limit_bytes=50 * 1024 * 1024
        ),
    )(
        node_latent, edge_latent, node_cot, edge_cot, edge_w1, edge_w2, node_w1, node_w2, spread
    )
    ew2, nw2 = ew2.T, nw2.T
    if not scatter:
        ew1, nw1 = (
            lax.psum_scatter(g, "dom", scatter_dimension=0, tiled=True) for g in (ew1, nw1)
        )
        ew2, nw2 = (
            lax.psum_scatter(g, "dom", scatter_dimension=1, tiled=True) for g in (ew2, nw2)
        )
    return node_grad, edge_grad, ew1, ew2, nw1, nw2


def solution(mesh):
    placed = (
        P(("groups", "dom"), None),
        P(("groups", "dom"), None),
        P(("groups", "dom"), None),
        P(("groups", "dom"), None),
        P(None, "mp"),
        P("mp", None),
        P(None, "mp"),
        P("mp", None),
        P("dom", None, None),
        P("dom"),
        P("dom"),
        P("dom"),
    )
    return jax.shard_map(
        functools.partial(local, mesh.shape["dom"]),
        mesh=mesh,
        in_specs=placed,
        out_specs=(
            P(("groups", "dom"), None),
            P(("groups", "dom"), None),
            P(("groups", "dom"), "mp"),
            P(("groups", "mp"), "dom"),
            P(("groups", "dom"), "mp"),
            P(("groups", "mp"), "dom"),
        ),
        check_vma=False,
    )
```

time: 410 us -> 55.6 us (0.14)
  waiting for transfers between devices: 324 us -> 0 us
  Pallas kernels: 0 us -> 42.9 us
  starting transfers between devices: 21.7 us -> 0 us
  matrix products: 17.2 us -> 0 us
  between operations: 15.4 us -> 1.41 us
  other arithmetic: 14 us -> 0.74 us
  local copies, waits for them, and re-layouts: 16.9 us -> 10.1 us
    reduce_scatter x4 -> x0, waiting for transfers between devices: 247 us -> none  [the longest x1 68.2 us: local(): lax.psum_scatter(weight_term(edge_input, edge_dpre), 'dom', scatter_dimen...]
    psum x4 -> x0, waiting for transfers between devices: 67.5 us -> none  [the longest x2 34.7 us: second_layer(): return lax.psum(partial_out.astype(jnp.bfloat16), 'mp').astype(jnp.float32)]
    pallas_call x0 -> x1, Pallas kernels: none -> 42.9 us  [local(): pl.pallas_call(functools.partial(kernel, (count, neigh, slots, scatter)),...]
    ppermute x12 -> x0, starting transfers between devices: 21.4 us -> none  [passed_along(): lax.ppermute(shard, axis, [(i, (i + by) % count) for i in range(count)])]
    dot_general x15 -> x0, matrix products: 17.2 us -> none  [the longest x4 7.35 us: contract_rows(): lax.dot_general(left, right, (((0,), (0,)), ((), ())), preferred_element_...]
    gather x4 -> x0, local copies, waits for them, and re-layouts: 9.81 us -> none  [the longest x1 2.75 us: local(): node_latent[edge_receiver]]
    ppermute x12 -> x0, waiting for transfers between devices: 9.29 us -> none  [passed_along(): lax.ppermute(shard, axis, [(i, (i + by) % count) for i in range(count)])]
    reduce_sum x6 -> x0, other arithmetic: 6.54 us -> none  [the longest x2 2.45 us: layer_norm(): inverse = lax.rsqrt(jnp.mean(center * center, axis=-1, keepdims=True) + EPS)]
  transfers between devices with their start and end apart: 20 -> 0, of which waited for: 11 -> 0; matrix products, arithmetic and copies ran while one was open for 5% -> 0% of each run, Pallas kernels for 0% -> 0%
where the time goes in v1:
time: 55.6 us; the launch traced here: 55.2 us
  Pallas kernels  42.9 us (77%)
  local copies, waits for them, and re-layouts  10.1 us (18%)
  between operations  1.41 us (3%)
  other arithmetic  0.74 us (1%)
    pallas_call x1, Pallas kernels, local(): pl.pallas_call(functools.partial(kernel, (count, neigh, slots, scatter)),...  42.9 us
    unnamed x22, local copies, waits for them, and re-layouts  10 us

profile of v1, /device:TPU:0, one launch (start us, length us, event | category | flops | bytes accessed | tf_op | source)
XLA Modules:
  0.0 55.2 jit_solution(13219487126072762305)
XLA Ops:
  0.6 0.0 copy-start.7
  0.6 0.0 copy-start.5
  1.3 0.0 copy-done.7
  1.4 0.1 reshape.15
  1.5 0.7 %add_select_fusion = (s32[576]{0:T(1024)S(1)}, s32[576]{0:T(1024)S(1)}) fusion(s32[576]{0:T(1024)} %param.22, s32[]{:T(128)} %bitcast.3, s32[576]{0:T(1024)} %param.21), kind=kLoop, calls=%fused_computation.1 | loop fusion | flops 2304 | bytes 9220 | tf_op jit(solution)/shard_map/jit(_where)/select_n | solution.py:387
  2.2 0.0 copy-done.5
  2.2 0.0 copy-start
  2.3 1.1 %copy-done = bf16[576,512]{1,0:T(8,128)(2,1)S(1)} copy-done((bf16[576,512]{1,0:T(8,128)(2,1)S(1)}, bf16[576,512]{1,0:T(8,128)(2,1)}, u32[]{:S(2)}) %copy-start) | copy-done | bytes 589848
  3.3 0.0 copy-start.1
  3.3 1.1 %copy-done.1 = bf16[576,512]{1,0:T(8,128)(2,1)S(1)} copy-done((bf16[576,512]{1,0:T(8,128)(2,1)S(1)}, bf16[576,512]{1,0:T(8,128)(2,1)}, u32[]{:S(2)}) %copy-start.1) | copy-done | bytes 589848
  4.4 0.0 copy-start.2
  4.4 1.0 %copy-done.2 = bf16[1024,256]{1,0:T(8,128)(2,1)S(1)} copy-done((bf16[1024,256]{1,0:T(8,128)(2,1)S(1)}, bf16[1024,256]{1,0:T(8,128)(2,1)}, u32[]{:S(2)}) %copy-start.2) | copy-done | bytes 524312
  5.4 0.0 copy-start.3
  5.4 0.9 %copy-done.3 = bf16[256,512]{1,0:T(8,128)(2,1)S(1)} copy-done((bf16[256,512]{1,0:T(8,128)(2,1)S(1)}, bf16[256,512]{1,0:T(8,128)(2,1)}, u32[]{:S(2)}) %copy-start.3) | copy-done | bytes 262168
  6.4 0.0 copy-start.4
  6.4 0.9 %copy-done.4 = bf16[256,512]{1,0:T(8,128)(2,1)S(1)} copy-done((bf16[256,512]{1,0:T(8,128)(2,1)S(1)}, bf16[256,512]{1,0:T(8,128)(2,1)}, u32[]{:S(2)}) %copy-start.4) | copy-done | bytes 262168
  7.3 0.0 copy-start.6
  7.3 0.9 %copy-done.6 = bf16[96,512]{1,0:T(8,128)(2,1)S(1)} copy-done((bf16[96,512]{1,0:T(8,128)(2,1)S(1)}, bf16[96,512]{1,0:T(8,128)(2,1)}, u32[]{:S(2)}) %copy-start.6) | copy-done | bytes 98328
  8.2 42.9 %shard_map.163 = (bf16[96,512]{1,0:T(8,128)(2,1)S(1)}, bf16[576,512]{1,0:T(8,128)(2,1)S(1)}, f32[192,256]{1,0:T(8,128)S(1)}, f32[64,256]{1,0:T(8,128)S(1)}, f32[...) custom-call(bf16[96,512]{1,0:T(8,128)(2,1)S(1)} %copy-done.5, bf16[576,512]{1,0:T(8,128)(2,1)S(1)} %copy-done, ...), custom_call_target="tpu_custom_call" | custom-call | tf_op jit(solution)/shard_map/pallas_call | solution.py:457
  51.1 0.6 %copy.25 = bf16[96,512]{1,0:T(8,128)(2,1)} copy(bf16[96,512]{1,0:T(8,128)(2,1)S(1)} %get-tuple-element.26) | data formatting | bytes 196608
  51.7 0.8 %copy.26 = bf16[576,512]{1,0:T(8,128)(2,1)} copy(bf16[576,512]{1,0:T(8,128)(2,1)S(1)} %get-tuple-element.27) | data formatting | bytes 1179648
  52.6 0.7 %copy.27 = f32[192,256]{1,0:T(8,128)} copy(f32[192,256]{1,0:T(8,128)S(1)} %get-tuple-element.28) | data formatting | bytes 393216
  53.2 0.6 %copy.28 = f32[256,64]{0,1:T(8,128)} copy(f32[256,64]{0,1:T(8,128)S(1)} %bitcast.5) | data formatting | bytes 131072
  53.9 0.7 %copy.29 = f32[128,256]{1,0:T(8,128)} copy(f32[128,256]{1,0:T(8,128)S(1)} %get-tuple-element.30) | data formatting | bytes 262144
  54.5 0.6 %copy.30 = f32[256,64]{0,1:T(8,128)} copy(f32[256,64]{0,1:T(8,128)S(1)} %bitcast.4) | data formatting | bytes 131072
  (9 shorter events, 0.1 us)
Async XLA Ops:
  0.6 0.7 %copy-start.7 = (s32[1,6,8]{2,0,1:T(1,128)S(1)}, s32[1,6,8]{2,0,1:T(1,128)}, u32[]{:S(2)}) copy-start(s32[1,6,8]{2,0,1:T(1,128)} %param.20) | copy-start | bytes 580
  0.6 1.6 %copy-start.5 = (bf16[96,512]{1,0:T(8,128)(2,1)S(1)}, bf16[96,512]{1,0:T(8,128)(2,1)}, u32[]{:S(2)}) copy-start(bf16[96,512]{1,0:T(8,128)(2,1)} %node_ref.1) | copy-start | bytes 294916
  2.2 1.1 %copy-start = (bf16[576,512]{1,0:T(8,128)(2,1)S(1)}, bf16[576,512]{1,0:T(8,128)(2,1)}, u32[]{:S(2)}) copy-start(bf16[576,512]{1,0:T(8,128)(2,1)} %edge_ref.1) | copy-start | bytes 1769476
  3.3 1.1 %copy-start.1 = (bf16[576,512]{1,0:T(8,128)(2,1)S(1)}, bf16[576,512]{1,0:T(8,128)(2,1)}, u32[]{:S(2)}) copy-start(bf16[576,512]{1,0:T(8,128)(2,1)} %ecot_ref.1) | copy-start | bytes 1769476
  4.4 1.0 %copy-start.2 = (bf16[1024,256]{1,0:T(8,128)(2,1)S(1)}, bf16[1024,256]{1,0:T(8,128)(2,1)}, u32[]{:S(2)}) copy-start(bf16[1024,256]{1,0:T(8,128)(2,1)} %nw1_ref.1) | copy-start | bytes 1572868
  5.4 0.9 %copy-start.3 = (bf16[256,512]{1,0:T(8,128)(2,1)S(1)}, bf16[256,512]{1,0:T(8,128)(2,1)}, u32[]{:S(2)}) copy-start(bf16[256,512]{1,0:T(8,128)(2,1)} %w2_ref.1) | copy-start | bytes 786436
  6.4 0.9 %copy-start.4 = (bf16[256,512]{1,0:T(8,128)(2,1)S(1)}, bf16[256,512]{1,0:T(8,128)(2,1)}, u32[]{:S(2)}) copy-start(bf16[256,512]{1,0:T(8,128)(2,1)} %nw2_ref.1) | copy-start | bytes 786436
  7.3 0.9 %copy-start.6 = (bf16[96,512]{1,0:T(8,128)(2,1)S(1)}, bf16[96,512]{1,0:T(8,128)(2,1)}, u32[]{:S(2)}) copy-start(bf16[96,512]{1,0:T(8,128)(2,1)} %ncot_ref.1) | copy-start | bytes 294916

commit v2 on v1

--- a/solution.py
+++ b/solution.py
@@ -12,6 +12,7 @@
 F32 = jnp.float32
 MESH = pl.DeviceIdType.MESH
 CHUNKS = 3
+VMEM_LIMIT = 62 * 1024 * 1024
 
 
 def dot(left, right, contract):
@@ -55,6 +56,30 @@
 
 def kernel(
     dims,
+    node_hbm,
+    edge_hbm,
+    ncot_hbm,
+    ecot_hbm,
+    w1_hbm,
+    w2_hbm,
+    nw1_hbm,
+    nw2_hbm,
+    send_hbm,
+    sender_hbm,
+    receiver_hbm,
+    count_ref,
+    ngrad_hbm,
+    egrad_hbm,
+    ew1_hbm,
+    ew2_hbm,
+    nw1_grad_hbm,
+    nw2_grad_hbm,
+    ngrad_ref,
+    egrad_ref,
+    ew1_out,
+    ew2_out,
+    nw1_out,
+    nw2_out,
     node_ref,
     edge_ref,
     ncot_ref,
@@ -63,13 +88,10 @@
     w2_ref,
     nw1_ref,
     nw2_ref,
-    codes_ref,
-    ngrad_ref,
-    egrad_ref,
-    ew1_out,
-    ew2_out,
-    nw1_out,
-    nw2_out,
+    send_ref,
+    sender_ref,
+    receiver_ref,
+    lists_ref,
     pick,
     pick_t,
     live,
@@ -119,6 +141,7 @@
     e1_r,
     e2_s,
     e2_r,
+    load_s,
 ):
     count, neigh, slots, scatter = dims
     me = lax.axis_index("dom")
@@ -145,6 +168,24 @@
             device_id_type=MESH,
         )
 
+    def load(index, src, dst):
+        copy = pltpu.make_async_copy(src, dst, load_s.at[index])
+        copy.start()
+        return copy
+
+    loads = [
+        load(0, send_hbm, send_ref),
+        load(1, node_hbm, node_ref),
+        load(2, sender_hbm, sender_ref),
+        load(3, receiver_hbm, receiver_ref),
+        load(4, edge_hbm, edge_ref),
+        load(5, w1_hbm, w1_ref),
+        load(6, w2_hbm, w2_ref),
+        load(7, nw1_hbm, nw1_ref),
+        load(8, nw2_hbm, nw2_ref),
+        load(9, ncot_hbm, ncot_ref),
+        load(10, ecot_hbm, ecot_ref),
+    ]
     barrier = pltpu.get_barrier_semaphore()
     shifts = sorted({offset_of(k, half) % count for k in range(neigh)})
     shifts = sorted(set(shifts) | {(-s) % count for s in shifts})
@@ -154,15 +195,22 @@
         pl.semaphore_signal(barrier, inc=1, device_id=at(shift), device_id_type=MESH)
     pl.semaphore_signal(barrier, inc=1, device_id=other, device_id_type=MESH)
 
-    spread = codes_ref[...]
-    place = lax.broadcasted_iota(jnp.int32, (pick.shape[0], spread.shape[1]), 0)
-    hit = (place == spread[0:1, :]) | (place == spread[1:2, :])
-    pick_f = jnp.where(hit, 1.0, 0.0).astype(F32)
-    pick[...] = pick_f[:, :edges].astype(BF)
-    send_place = lax.broadcasted_iota(jnp.int32, (nodes, listed), 0)
-    lists = jnp.where(send_place == spread[2:3, :listed], 1.0, 0.0).astype(F32).astype(BF)
+    send_place = lax.broadcasted_iota(jnp.int32, (nodes, slots), 0)
+    loads[0].wait()
+    for k in range(neigh):
+        hit = send_place == send_ref[k]
+        lists_ref[:, k * slots : (k + 1) * slots] = jnp.where(hit, 1.0, 0.0).astype(F32)
+    lists = lists_ref[...].astype(BF)
+    loads[1].wait()
     node = node_ref[...]
     halo_out[...] = tn(lists, node)
+    loads[2].wait()
+    loads[3].wait()
+    place = lax.broadcasted_iota(jnp.int32, pick.shape, 0)
+    alive = lax.broadcasted_iota(jnp.int32, pick.shape, 1) < count_ref[0]
+    hit = (place == sender_ref[...][None, :]) | (place == receiver_ref[...][None, :] + codes)
+    pick_f = jnp.where(hit & alive, 1.0, 0.0).astype(F32)
+    pick[...] = pick_f.astype(BF)
 
     pl.semaphore_wait(barrier, len(shifts) + 1)
     halo = []
@@ -175,9 +223,11 @@
         copy.start()
         halo.append(copy)
 
-    picked = jnp.transpose(pick_f)[:edges]
+    picked = jnp.transpose(pick_f)
     pick_t[...] = picked.astype(BF)
     live[...] = jnp.max(picked, axis=1, keepdims=True)
+    loads[4].wait()
+    loads[5].wait()
     pre[...] = nn(edge_ref[...], w1_ref[0:width])
     table[0:nodes] = nn(node, w1_ref[width : 2 * width]).astype(BF)
     table[codes : codes + nodes] = nn(node, w1_ref[2 * width : 3 * width]).astype(BF)
@@ -190,6 +240,7 @@
     sources[nodes:codes] = arrived
     table[nodes:codes] = nn(arrived, w1_ref[width : 2 * width]).astype(BF)
 
+    loads[6].wait()
     trades = []
     for c in range(CHUNKS):
         r = pl.ds(c * rows, rows)
@@ -202,6 +253,8 @@
         copy = remote(mine.at[r], theirs.at[r], mp_s.at[c], mp_r.at[c], other)
         copy.start()
         trades.append(copy)
+    for copy in loads[7:]:
+        copy.wait()
     node_first = nn(node, nw1_ref[0:width])
     for c in range(CHUNKS):
         r = pl.ds(c * rows, rows)
@@ -227,13 +280,10 @@
     trade.start()
     trades.append(trade)
 
-    pairs = count // 2
     x = lax.rem(me, 2)
     z = lax.div(me, 2)
-    order = list(range(1, pairs)) + [0]
-
-    def turn(k):
-        return lax.rem(z + k, pairs)
+    near = z + 1 - 2 * lax.rem(z, 2)
+    turns = [lax.rem(near + 2, 4), near, lax.rem(z + 2, 4), z]
 
     def place_slices(buf, first, second):
         a = first.shape[0] // count
@@ -242,36 +292,37 @@
             buf[j % 2, j // 2, 0:a] = first[j * a : (j + 1) * a].astype(BF)
             buf[j % 2, j // 2, a : a + b] = second[j * b : (j + 1) * b].astype(BF)
 
-    def first_phase(buf, land, send, recv):
-        copies = {}
-        for k in order:
-            copies[k] = remote(
-                buf.at[1 - x, turn(k)], land.at[turn(k)], send.at[k], recv.at[k],
+    def across_x(buf, land, send, recv):
+        copies = []
+        for k in range(4):
+            copy = remote(
+                buf.at[1 - x, turns[k]], land.at[k], send.at[k], recv.at[k],
                 {"dom": me + 1 - 2 * x},
             )
-            copies[k].start()
+            copy.start()
+            copies.append(copy)
         return copies
 
-    def second_phase(copies, buf, land, summed, land2, send, recv):
-        later = []
-        for k in range(1, pairs):
-            copies[k].wait_recv()
-            total = buf[x, turn(k)].astype(F32) + land[turn(k)].astype(F32)
-            summed[k - 1] = total.astype(BF)
-            copy = remote(
-                summed.at[k - 1], land2.at[k - 1], send.at[k - 1], recv.at[k - 1],
-                {"dom": turn(k) * 2 + x},
-            )
-            copy.start()
-            later.append(copy)
-        return later
-
-    def finish(copies, later, buf, land, land2, out_a, out_b):
-        copies[0].wait_recv()
-        total = buf[x, z].astype(F32) + land[z].astype(F32)
-        for k in range(1, pairs):
-            later[k - 1].wait_recv()
-            total = total + land2[k - 1].astype(F32)
+    def along_z(k, copies, buf, land, summed, land2, send, recv):
+        copies[k].wait_recv()
+        total = buf[x, turns[k]].astype(F32) + land[k].astype(F32)
+        if k == 2:
+            copies[4].wait_recv()
+            total = total + land2[0].astype(F32)
+        summed[k] = total.astype(BF)
+        copy = remote(
+            summed.at[k], land2.at[k], send.at[k], recv.at[k],
+            {"dom": (near if k < 2 else turns[2]) * 2 + x},
+        )
+        copy.start()
+        copies.append(copy)
+
+    def finish(copies, buf, land, summed, land2, out_a, out_b):
+        copies[3].wait_recv()
+        copies[5].wait_recv()
+        total = buf[x, z].astype(F32) + land[3].astype(F32) + land2[1].astype(F32)
+        copies[6].wait_recv()
+        total = total + land2[2].astype(F32)
         a = out_a.shape[0]
         out_a[...] = total[:a]
         out_b[...] = total[a:]
@@ -280,7 +331,8 @@
     node_w2_grad = tn(node_dout, node_act)
     if scatter:
         place_slices(nbuf, node_w1_grad, node_w2_grad)
-        n_first = first_phase(nbuf, np1, n1_s, n1_r)
+        n_copies = across_x(nbuf, np1, n1_s, n1_r)
+        n_rest = (n_copies, nbuf, np1, nsum, np2)
     else:
         nw1_out[...] = node_w1_grad
         nw2_out[...] = node_w2_grad
@@ -296,8 +348,8 @@
         d = norm_back(normed[r], inverse[r], upstream).astype(BF)
         dout[r] = d
         dpre[r] = (nt(d, w2_ref[...]) * slope[r]).astype(BF)
-    if scatter:
-        n_later = second_phase(n_first, nbuf, np1, nsum, np2, n2_s, n2_r)
+        if scatter and c > 0:
+            along_z(c - 1, *n_rest, n2_s, n2_r)
     sums = nn(pick[...], dpre[...]).astype(BF)
     by_code = sums[0:codes]
     by_node = sums[codes : codes + nodes]
@@ -307,7 +359,9 @@
     edge_w2_grad = tn(dout[...], act[...])
     if scatter:
         place_slices(ebuf, edge_w1_grad, edge_w2_grad)
-        e_first = first_phase(ebuf, ep1, e1_s, e1_r)
+        e_copies = across_x(ebuf, ep1, e1_s, e1_r)
+        e_rest = (e_copies, ebuf, ep1, esum, ep2)
+        along_z(2, *n_rest, n2_s, n2_r)
     else:
         ew1_out[...] = edge_w1_grad
         ew2_out[...] = edge_w2_grad
@@ -333,27 +387,62 @@
         edge_trades.append(copy)
     node_own = node_own + per_code[0:nodes] + nt(by_node, w1_ref[2 * width : 3 * width])
     if scatter:
-        e_later = second_phase(e_first, ebuf, ep1, esum, ep2, e2_s, e2_r)
+        along_z(0, *e_rest, e2_s, e2_r)
     for copy in backs:
         copy.wait_recv()
     fmine[...] = node_own + nn(lists, back_in[...].astype(BF))
     last = 2 * CHUNKS + 2
     final = remote(fmine, ftheirs, mp_s.at[last], mp_r.at[last], other)
     final.start()
+    if scatter:
+        along_z(1, *e_rest, e2_s, e2_r)
     for c in range(CHUNKS):
         r = pl.ds(c * rows, rows)
         edge_trades[c].wait_recv()
         total = dmine[r].astype(F32) + dtheirs[r].astype(F32)
         egrad_ref[r] = (live[r] * (ecot_ref[r].astype(F32) + total)).astype(BF)
+    if scatter:
+        along_z(2, *e_rest, e2_s, e2_r)
+    stores = [load(12, egrad_ref, egrad_hbm)]
     final.wait_recv()
     ngrad_ref[...] = (ncot_ref[...].astype(F32) + fmine[...] + ftheirs[...]).astype(BF)
-    if scatter:
-        finish(n_first, n_later, nbuf, np1, np2, nw1_out, nw2_out)
-        finish(e_first, e_later, ebuf, ep1, ep2, ew1_out, ew2_out)
-        for copy in list(n_first.values()) + n_later + list(e_first.values()) + e_later:
+    stores.append(load(11, ngrad_ref, ngrad_hbm))
+    if scatter:
+        finish(*n_rest, nw1_out, nw2_out)
+    stores.append(load(15, nw1_out, nw1_grad_hbm))
+    stores.append(load(16, nw2_out, nw2_grad_hbm))
+    if scatter:
+        finish(*e_rest, ew1_out, ew2_out)
+    stores.append(load(13, ew1_out, ew1_hbm))
+    stores.append(load(14, ew2_out, ew2_hbm))
+    if scatter:
+        for copy in n_copies + e_copies:
             copy.wait_send()
     for copy in halo + trades + backs + edge_trades + [final]:
         copy.wait_send()
+    for copy in stores:
+        copy.wait()
+
+
+def write_kernel(*refs):
+    copies = []
+    for index in range(6):
+        copy = pltpu.make_async_copy(refs[index], refs[6 + index], refs[12].at[index])
+        copy.start()
+        copies.append(copy)
+    for copy in copies:
+        copy.wait()
+
+
+def write_out(*results):
+    return pl.pallas_call(
+        write_kernel,
+        out_shape=[jax.ShapeDtypeStruct(v.shape, v.dtype) for v in results],
+        in_specs=[pl.BlockSpec(memory_space=pltpu.HBM)] * 6,
+        out_specs=[pl.BlockSpec(memory_space=pltpu.HBM)] * 6,
+        scratch_shapes=[pltpu.SemaphoreType.DMA((6,))],
+        compiler_params=pltpu.CompilerParams(vmem_limit_bytes=VMEM_LIMIT),
+    )(*results)
 
 
 def local(
@@ -378,31 +467,31 @@
     listed = neigh * slots
     codes = nodes + listed
     total = -(-(codes + nodes) // 128) * 128
-    padded = -(-edges // 128) * 128
-    live = jnp.arange(edges, dtype=jnp.int32) < edge_count[0]
-    fill = padded - edges
-    spread = jnp.stack(
-        [
-            jnp.pad(jnp.where(live, edge_sender, -1), (0, fill), constant_values=-1),
-            jnp.pad(jnp.where(live, edge_receiver + codes, -1), (0, fill), constant_values=-1),
-            jnp.pad(send_rows.reshape(-1), (0, padded - listed), constant_values=-1),
-        ]
-    )
-    spread = jnp.pad(spread, ((0, 5), (0, 0)), constant_values=-1)
     w1_rows, nw1_rows = edge_w1.shape[0], node_w1.shape[0]
     scatter = (
-        count % 2 == 0
+        count == 8
         and w1_rows % (16 * count) == 0
         and nw1_rows % (16 * count) == 0
         and width % (16 * count) == 0
     )
     parts = count if scatter else 1
-    pairs = max(count // 2, 2) if scatter else 2
     n_rows = (nw1_rows + width) // parts if scatter else 16
     e_rows = (w1_rows + width) // parts if scatter else 16
     vmem = pltpu.VMEM
     dma = pltpu.SemaphoreType.DMA
     scratch = [
+        vmem((nodes, width), BF),
+        vmem((edges, width), BF),
+        vmem((nodes, width), BF),
+        vmem((edges, width), BF),
+        vmem(edge_w1.shape, BF),
+        vmem(edge_w2.shape, BF),
+        vmem(node_w1.shape, BF),
+        vmem(node_w2.shape, BF),
+        vmem((neigh, 1, slots), jnp.int32),
+        vmem((edges,), jnp.int32),
+        vmem((edges,), jnp.int32),
+        vmem((nodes, listed), F32),
         vmem((total, edges), BF),
         vmem((edges, total), BF),
         vmem((edges, 1), F32),
@@ -430,57 +519,61 @@
         vmem((listed, width), F32),
         vmem((nodes, width), F32),
         vmem((nodes, width), F32),
-        vmem((2, pairs, n_rows, hidden), BF),
-        vmem((pairs, n_rows, hidden), BF),
-        vmem((pairs - 1, n_rows, hidden), BF),
-        vmem((pairs - 1, n_rows, hidden), BF),
-        vmem((2, pairs, e_rows, hidden), BF),
-        vmem((pairs, e_rows, hidden), BF),
-        vmem((pairs - 1, e_rows, hidden), BF),
-        vmem((pairs - 1, e_rows, hidden), BF),
+        vmem((2, 4, n_rows, hidden), BF),
+        vmem((4, n_rows, hidden), BF),
+        vmem((3, n_rows, hidden), BF),
+        vmem((3, n_rows, hidden), BF),
+        vmem((2, 4, e_rows, hidden), BF),
+        vmem((4, e_rows, hidden), BF),
+        vmem((3, e_rows, hidden), BF),
+        vmem((3, e_rows, hidden), BF),
         dma((neigh,)),
         dma((neigh,)),
         dma((neigh,)),
         dma((neigh,)),
         dma((2 * CHUNKS + 3,)),
         dma((2 * CHUNKS + 3,)),
-        dma((pairs,)),
-        dma((pairs,)),
-        dma((pairs - 1,)),
-        dma((pairs - 1,)),
-        dma((pairs,)),
-        dma((pairs,)),
-        dma((pairs - 1,)),
-        dma((pairs - 1,)),
+        dma((4,)),
+        dma((4,)),
+        dma((3,)),
+        dma((3,)),
+        dma((4,)),
+        dma((4,)),
+        dma((3,)),
+        dma((3,)),
+        dma((17,)),
     ]
     shape = jax.ShapeDtypeStruct
+    shapes = (
+        shape((nodes, width), BF),
+        shape((edges, width), BF),
+        shape((w1_rows // parts, hidden), F32),
+        shape((width // parts, hidden), F32),
+        shape((nw1_rows // parts, hidden), F32),
+        shape((width // parts, hidden), F32),
+    )
     node_grad, edge_grad, ew1, ew2, nw1, nw2 = pl.pallas_call(
         functools.partial(kernel, (count, neigh, slots, scatter)),
-        out_shape=(
-            shape((nodes, width), BF),
-            shape((edges, width), BF),
-            shape((w1_rows // parts, hidden), F32),
-            shape((width // parts, hidden), F32),
-            shape((nw1_rows // parts, hidden), F32),
-            shape((width // parts, hidden), F32),
-        ),
-        in_specs=[pl.BlockSpec(memory_space=pltpu.VMEM)] * 9,
-        out_specs=[pl.BlockSpec(memory_space=pltpu.VMEM)] * 6,
-        scratch_shapes=scratch,
+        out_shape=shapes,
+        in_specs=[pl.BlockSpec(memory_space=pltpu.HBM)] * 11
+        + [pl.BlockSpec(memory_space=pltpu.SMEM)],
+        out_specs=[pl.BlockSpec(memory_space=pltpu.HBM)] * 6,
+        scratch_shapes=[vmem(v.shape, v.dtype) for v in shapes] + scratch,
         compiler_params=pltpu.CompilerParams(
-            collective_id=0, has_side_effects=True, vmem_limit_bytes=50 * 1024 * 1024
+            collective_id=0, has_side_effects=True, vmem_limit_bytes=VMEM_LIMIT
         ),
     )(
-        node_latent, edge_latent, node_cot, edge_cot, edge_w1, edge_w2, node_w1, node_w2, spread
+        node_latent, edge_latent, node_cot, edge_cot, edge_w1, edge_w2, node_w1, node_w2,
+        jnp.transpose(send_rows, (1, 0, 2)), edge_sender, edge_receiver, edge_count,
     )
+    if scatter:
+        node_grad, edge_grad, ew1, ew2, nw1, nw2 = write_out(
+            node_grad, edge_grad, ew1, ew2, nw1, nw2
+        )
+        return node_grad, edge_grad, ew1, ew2.T, nw1, nw2.T
     ew2, nw2 = ew2.T, nw2.T
-    if not scatter:
-        ew1, nw1 = (
-            lax.psum_scatter(g, "dom", scatter_dimension=0, tiled=True) for g in (ew1, nw1)
-        )
-        ew2, nw2 = (
-            lax.psum_scatter(g, "dom", scatter_dimension=1, tiled=True) for g in (ew2, nw2)
-        )
+    ew1, nw1 = (lax.psum_scatter(g, "dom", scatter_dimension=0, tiled=True) for g in (ew1, nw1))
+    ew2, nw2 = (lax.psum_scatter(g, "dom", scatter_dimension=1, tiled=True) for g in (ew2, nw2))
     return node_grad, edge_grad, ew1, ew2, nw1, nw2
 
 

time: 55.6 us -> 83 us (1.49)
  Pallas kernels: 42.9 us -> 81.6 us
  local copies, waits for them, and re-layouts: 10.1 us -> 0 us
    pallas_call x0 -> x1, Pallas kernels: none -> 35.9 us  [write_out(): pl.pallas_call(write_kernel, out_shape=[jax.ShapeDtypeStruct(v.shape, v.d...]
    unnamed x22 -> x0, local copies, waits for them, and re-layouts: 10 us -> none
    pallas_call x1, Pallas kernels: 42.9 us -> 45.7 us  [local(): pl.pallas_call(functools.partial(kernel, (count, neigh, slots, scatter)),...]
where the time goes in v2:
time: 83 us; the launch traced here: 82.8 us
  Pallas kernels  81.6 us (98%)
  between operations  1.29 us (2%)
    pallas_call x1, Pallas kernels, local(): pl.pallas_call(functools.partial(kernel, (count, neigh, slots, scatter)),...  45.7 us
    pallas_call x1, Pallas kernels, write_out(): pl.pallas_call(write_kernel, out_shape=[jax.ShapeDtypeStruct(v.shape, v.d...  35.9 us

profile of v2, /device:TPU:0, one launch (start us, length us, event | category | flops | bytes accessed | tf_op | source)
XLA Modules:
  0.0 82.8 jit_solution(11625584072218172470)
XLA Ops:
  1.3 45.7 %shard_map.163 = (bf16[96,512]{1,0:T(8,128)(2,1)}, bf16[576,512]{1,0:T(8,128)(2,1)}, f32[192,256]{1,0:T(8,128)}, f32[64,256]{1,0:T(8,128)}, f32[128,256]{1,0:T(8,128)}, /*index=5*/f32[64,256]{1,0:T(8,128)}) custom-call(bf16[96,512]{1,0:T(8,128)(2,1)} %node_hbm.1, bf16[576,512]{1,0:T(8,128)(2,1)} %edge_hbm.1, bf16[96,512]{1,0:T(8,128)(2,1)} %ncot_hbm.1, ...), custom_call_target="tpu_custom_call" | custom-call | tf_op jit(solution)/shard_map/pallas_call | solution.py:555
  46.9 35.9 %shard_map.164 = (bf16[96,512]{1,0:T(8,128)(2,1)}, bf16[576,512]{1,0:T(8,128)(2,1)}, f32[192,256]{1,0:T(8,128)}, f32[64,256]{1,0:T(8,128)}, f32[128,256]{1,0:T(8,128)}, /*index=5*/f32[64,256]{1,0:T(8,128)}) custom-call(bf16[96,512]{1,0:T(8,128)(2,1)} %get-tuple-element.18.refs_0_, bf16[576,512]{1,0:T(8,128)(2,1)} %get-tuple-element.19.refs_1_, ...), custom_call_target="tpu_custom_call" | custom-call | tf_op jit(solution)/shard_map/pallas_call | solution.py:438

commit v3 on v2

--- a/solution.py
+++ b/solution.py
@@ -119,28 +119,15 @@
     back_in,
     fmine,
     ftheirs,
-    nbuf,
-    np1,
-    nsum,
-    np2,
-    ebuf,
-    ep1,
-    esum,
-    ep2,
+    rs_refs,
     halo_s,
     halo_r,
     back_s,
     back_r,
     mp_s,
     mp_r,
-    n1_s,
-    n1_r,
-    n2_s,
-    n2_r,
-    e1_s,
-    e1_r,
-    e2_s,
-    e2_r,
+    rs_s,
+    rs_r,
     load_s,
 ):
     count, neigh, slots, scatter = dims
@@ -283,56 +270,72 @@
     x = lax.rem(me, 2)
     z = lax.div(me, 2)
     near = z + 1 - 2 * lax.rem(z, 2)
-    turns = [lax.rem(near + 2, 4), near, lax.rem(z + 2, 4), z]
-
-    def place_slices(buf, first, second):
-        a = first.shape[0] // count
-        b = second.shape[0] // count
+    far = lax.rem(z + 2, 4)
+    both = lax.rem(near + 2, 4)
+
+    def spot(flips):
+        along = {"": z, "0": near, "1": far, "01": both}
+        return (1 - x if "x" in flips else x), along["".join(sorted(set(flips) - {"x"}))]
+
+    def device(flips):
+        across, along = spot(flips)
+        return {"dom": along * 2 + across}
+
+    routes = ("x01", "0x1", "x01", "0x1")
+
+    def owners(which):
+        first, second, third = routes[which]
+        return first, second, third, (second + third, second, third, "")
+
+    def first_hop(which, grad):
+        buf, land = rs_refs[which][:2]
+        size = grad.shape[0] // count
         for j in range(count):
-            buf[j % 2, j // 2, 0:a] = first[j * a : (j + 1) * a].astype(BF)
-            buf[j % 2, j // 2, a : a + b] = second[j * b : (j + 1) * b].astype(BF)
-
-    def across_x(buf, land, send, recv):
+            buf[j % 2, j // 2] = grad[j * size : (j + 1) * size].astype(BF)
+        first, _, _, slices = owners(which)
         copies = []
         for k in range(4):
             copy = remote(
-                buf.at[1 - x, turns[k]], land.at[k], send.at[k], recv.at[k],
-                {"dom": me + 1 - 2 * x},
+                buf.at[spot(first + slices[k])], land.at[k],
+                rs_s.at[which, k], rs_r.at[which, k], device(first),
             )
             copy.start()
             copies.append(copy)
-        return copies
-
-    def along_z(k, copies, buf, land, summed, land2, send, recv):
+        sums[which] = copies
+
+    def next_hop(which, k):
+        copies = sums[which]
+        buf, land, summed, land2 = rs_refs[which]
+        _, second, third, slices = owners(which)
         copies[k].wait_recv()
-        total = buf[x, turns[k]].astype(F32) + land[k].astype(F32)
+        total = buf[spot(slices[k])].astype(F32) + land[k].astype(F32)
         if k == 2:
             copies[4].wait_recv()
             total = total + land2[0].astype(F32)
         summed[k] = total.astype(BF)
         copy = remote(
-            summed.at[k], land2.at[k], send.at[k], recv.at[k],
-            {"dom": (near if k < 2 else turns[2]) * 2 + x},
+            summed.at[k], land2.at[k], rs_s.at[which, 4 + k], rs_r.at[which, 4 + k],
+            device(second if k < 2 else third),
         )
         copy.start()
         copies.append(copy)
 
-    def finish(copies, buf, land, summed, land2, out_a, out_b):
+    def finish(which, out):
+        copies = sums[which]
+        buf, land, summed, land2 = rs_refs[which]
         copies[3].wait_recv()
         copies[5].wait_recv()
         total = buf[x, z].astype(F32) + land[3].astype(F32) + land2[1].astype(F32)
         copies[6].wait_recv()
-        total = total + land2[2].astype(F32)
-        a = out_a.shape[0]
-        out_a[...] = total[:a]
-        out_b[...] = total[a:]
-
+        out[...] = total + land2[2].astype(F32)
+
+    sums = {}
+    node_w2_grad = tn(node_dout, node_act)
+    if scatter:
+        first_hop(1, node_w2_grad)
     node_w1_grad = jnp.concatenate([tn(node, node_dpre), tn(gathered, node_dpre)], axis=0)
-    node_w2_grad = tn(node_dout, node_act)
-    if scatter:
-        place_slices(nbuf, node_w1_grad, node_w2_grad)
-        n_copies = across_x(nbuf, np1, n1_s, n1_r)
-        n_rest = (n_copies, nbuf, np1, nsum, np2)
+    if scatter:
+        first_hop(0, node_w1_grad)
     else:
         nw1_out[...] = node_w1_grad
         nw2_out[...] = node_w2_grad
@@ -349,19 +352,21 @@
         dout[r] = d
         dpre[r] = (nt(d, w2_ref[...]) * slope[r]).astype(BF)
         if scatter and c > 0:
-            along_z(c - 1, *n_rest, n2_s, n2_r)
-    sums = nn(pick[...], dpre[...]).astype(BF)
-    by_code = sums[0:codes]
-    by_node = sums[codes : codes + nodes]
+            next_hop(1, c - 1)
+            next_hop(0, c - 1)
+    edge_w2_grad = tn(dout[...], act[...])
+    if scatter:
+        first_hop(3, edge_w2_grad)
+    merged = nn(pick[...], dpre[...]).astype(BF)
+    by_code = merged[0:codes]
+    by_node = merged[codes : codes + nodes]
     edge_w1_grad = jnp.concatenate(
         [tn(edge_ref[...], dpre[...]), tn(sources[...], by_code), tn(node, by_node)], axis=0
     )
-    edge_w2_grad = tn(dout[...], act[...])
-    if scatter:
-        place_slices(ebuf, edge_w1_grad, edge_w2_grad)
-        e_copies = across_x(ebuf, ep1, e1_s, e1_r)
-        e_rest = (e_copies, ebuf, ep1, esum, ep2)
-        along_z(2, *n_rest, n2_s, n2_r)
+    if scatter:
+        first_hop(2, edge_w1_grad)
+        next_hop(1, 2)
+        next_hop(0, 2)
     else:
         ew1_out[...] = edge_w1_grad
         ew2_out[...] = edge_w2_grad
@@ -387,7 +392,8 @@
         edge_trades.append(copy)
     node_own = node_own + per_code[0:nodes] + nt(by_node, w1_ref[2 * width : 3 * width])
     if scatter:
-        along_z(0, *e_rest, e2_s, e2_r)
+        next_hop(3, 0)
+        next_hop(2, 0)
     for copy in backs:
         copy.wait_recv()
     fmine[...] = node_own + nn(lists, back_in[...].astype(BF))
@@ -395,28 +401,32 @@
     final = remote(fmine, ftheirs, mp_s.at[last], mp_r.at[last], other)
     final.start()
     if scatter:
-        along_z(1, *e_rest, e2_s, e2_r)
+        next_hop(3, 1)
+        next_hop(2, 1)
     for c in range(CHUNKS):
         r = pl.ds(c * rows, rows)
         edge_trades[c].wait_recv()
         total = dmine[r].astype(F32) + dtheirs[r].astype(F32)
         egrad_ref[r] = (live[r] * (ecot_ref[r].astype(F32) + total)).astype(BF)
     if scatter:
-        along_z(2, *e_rest, e2_s, e2_r)
+        next_hop(3, 2)
+        next_hop(2, 2)
     stores = [load(12, egrad_ref, egrad_hbm)]
     final.wait_recv()
     ngrad_ref[...] = (ncot_ref[...].astype(F32) + fmine[...] + ftheirs[...]).astype(BF)
     stores.append(load(11, ngrad_ref, ngrad_hbm))
     if scatter:
-        finish(*n_rest, nw1_out, nw2_out)
+        finish(1, nw2_out)
+        finish(0, nw1_out)
     stores.append(load(15, nw1_out, nw1_grad_hbm))
     stores.append(load(16, nw2_out, nw2_grad_hbm))
     if scatter:
-        finish(*e_rest, ew1_out, ew2_out)
+        finish(3, ew2_out)
+        finish(2, ew1_out)
     stores.append(load(13, ew1_out, ew1_hbm))
     stores.append(load(14, ew2_out, ew2_hbm))
     if scatter:
-        for copy in n_copies + e_copies:
+        for copy in sums[0] + sums[1] + sums[2] + sums[3]:
             copy.wait_send()
     for copy in halo + trades + backs + edge_trades + [final]:
         copy.wait_send()
@@ -425,13 +435,20 @@
 
 
 def write_kernel(*refs):
-    copies = []
-    for index in range(6):
-        copy = pltpu.make_async_copy(refs[index], refs[6 + index], refs[12].at[index])
-        copy.start()
-        copies.append(copy)
-    for copy in copies:
-        copy.wait()
+    ins, outs, held, sems = refs[:6], refs[6:12], refs[12:18], refs[18]
+    order = (1, 2, 4, 0, 3, 5)
+    copies = {}
+    for index in order:
+        copies[index] = pltpu.make_async_copy(ins[index], held[index], sems.at[0, index])
+        copies[index].start()
+    stores = []
+    for index in order:
+        copies[index].wait()
+        store = pltpu.make_async_copy(held[index], outs[index], sems.at[1, index])
+        store.start()
+        stores.append(store)
+    for store in stores:
+        store.wait()
 
 
 def write_out(*results):
@@ -440,7 +457,8 @@
         out_shape=[jax.ShapeDtypeStruct(v.shape, v.dtype) for v in results],
         in_specs=[pl.BlockSpec(memory_space=pltpu.HBM)] * 6,
         out_specs=[pl.BlockSpec(memory_space=pltpu.HBM)] * 6,
-        scratch_shapes=[pltpu.SemaphoreType.DMA((6,))],
+        scratch_shapes=[pltpu.VMEM(v.shape, v.dtype) for v in results]
+        + [pltpu.SemaphoreType.DMA((2, 6))],
         compiler_params=pltpu.CompilerParams(vmem_limit_bytes=VMEM_LIMIT),
     )(*results)
 
@@ -475,8 +493,7 @@
         and width % (16 * count) == 0
     )
     parts = count if scatter else 1
-    n_rows = (nw1_rows + width) // parts if scatter else 16
-    e_rows = (w1_rows + width) // parts if scatter else 16
+    sizes = [r // parts if scatter else 16 for r in (nw1_rows, width, w1_rows, width)]
     vmem = pltpu.VMEM
     dma = pltpu.SemaphoreType.DMA
     scratch = [
@@ -519,28 +536,23 @@
         vmem((listed, width), F32),
         vmem((nodes, width), F32),
         vmem((nodes, width), F32),
-        vmem((2, 4, n_rows, hidden), BF),
-        vmem((4, n_rows, hidden), BF),
-        vmem((3, n_rows, hidden), BF),
-        vmem((3, n_rows, hidden), BF),
-        vmem((2, 4, e_rows, hidden), BF),
-        vmem((4, e_rows, hidden), BF),
-        vmem((3, e_rows, hidden), BF),
-        vmem((3, e_rows, hidden), BF),
+        [
+            (
+                vmem((2, 4, size, hidden), BF),
+                vmem((4, size, hidden), BF),
+                vmem((3, size, hidden), BF),
+                vmem((3, size, hidden), BF),
+            )
+            for size in sizes
+        ],
         dma((neigh,)),
         dma((neigh,)),
         dma((neigh,)),
         dma((neigh,)),
         dma((2 * CHUNKS + 3,)),
         dma((2 * CHUNKS + 3,)),
-        dma((4,)),
-        dma((4,)),
-        dma((3,)),
-        dma((3,)),
-        dma((4,)),
-        dma((4,)),
-        dma((3,)),
-        dma((3,)),
+        dma((4, 7)),
+        dma((4, 7)),
         dma((17,)),
     ]
     shape = jax.ShapeDtypeStruct

time: 83 us -> 46.6 us (0.56)
  Pallas kernels: 81.6 us -> 45.2 us
    pallas_call x1, Pallas kernels: 35.9 us -> 2.16 us  [write_out(): pl.pallas_call(write_kernel, out_shape=[jax.ShapeDtypeStruct(v.shape, v.d...]
    pallas_call x1, Pallas kernels: 45.7 us -> 43 us  [local(): pl.pallas_call(functools.partial(kernel, (count, neigh, slots, scatter)),...]
where the time goes in v3:
time: 46.6 us; the launch traced here: 46.4 us
  Pallas kernels  45.2 us (97%)
  between operations  1.29 us (3%)
    pallas_call x1, Pallas kernels, local(): pl.pallas_call(functools.partial(kernel, (count, neigh, slots, scatter)),...  43 us
    pallas_call x1, Pallas kernels, write_out(): pl.pallas_call(write_kernel, out_shape=[jax.ShapeDtypeStruct(v.shape, v.d...  2.16 us

profile of v3, /device:TPU:0, one launch (start us, length us, event | category | flops | bytes accessed | tf_op | source)
XLA Modules:
  0.0 46.4 jit_solution(10192617811171231265)
XLA Ops:
  1.3 43.0 %shard_map.163 = (bf16[96,512]{1,0:T(8,128)(2,1)}, bf16[576,512]{1,0:T(8,128)(2,1)}, f32[192,256]{1,0:T(8,128)}, f32[64,256]{1,0:T(8,128)}, f32[128,256]{1,0:T(8,128)}, /*index=5*/f32[64,256]{1,0:T(8,128)}) custom-call(bf16[96,512]{1,0:T(8,128)(2,1)} %node_hbm.1, bf16[576,512]{1,0:T(8,128)(2,1)} %edge_hbm.1, bf16[96,512]{1,0:T(8,128)(2,1)} %ncot_hbm.1, ...), custom_call_target="tpu_custom_call" | custom-call | tf_op jit(solution)/shard_map/pallas_call | solution.py:567
  44.3 2.2 %shard_map.164 = (bf16[96,512]{1,0:T(8,128)(2,1)}, bf16[576,512]{1,0:T(8,128)(2,1)}, f32[192,256]{1,0:T(8,128)}, f32[64,256]{1,0:T(8,128)}, f32[128,256]{1,0:T(8,128)}, /*index=5*/f32[64,256]{1,0:T(8,128)}) custom-call(bf16[96,512]{1,0:T(8,128)(2,1)} %get-tuple-element.18.refs_0_, bf16[576,512]{1,0:T(8,128)(2,1)} %get-tuple-element.19.refs_1_, ...), custom_call_target="tpu_custom_call" | custom-call | tf_op jit(solution)/shard_map/pallas_call | solution.py:455

commit v4 on v3

--- a/solution.py
+++ b/solution.py
@@ -360,17 +360,6 @@
     merged = nn(pick[...], dpre[...]).astype(BF)
     by_code = merged[0:codes]
     by_node = merged[codes : codes + nodes]
-    edge_w1_grad = jnp.concatenate(
-        [tn(edge_ref[...], dpre[...]), tn(sources[...], by_code), tn(node, by_node)], axis=0
-    )
-    if scatter:
-        first_hop(2, edge_w1_grad)
-        next_hop(1, 2)
-        next_hop(0, 2)
-    else:
-        ew1_out[...] = edge_w1_grad
-        ew2_out[...] = edge_w2_grad
-
     per_code = nt(by_code, w1_ref[width : 2 * width])
     back_out[...] = per_code[nodes:codes]
     backs = []
@@ -382,6 +371,17 @@
         )
         copy.start()
         backs.append(copy)
+    edge_w1_grad = jnp.concatenate(
+        [tn(edge_ref[...], dpre[...]), tn(sources[...], by_code), tn(node, by_node)], axis=0
+    )
+    if scatter:
+        first_hop(2, edge_w1_grad)
+        next_hop(1, 2)
+        next_hop(0, 2)
+    else:
+        ew1_out[...] = edge_w1_grad
+        ew2_out[...] = edge_w2_grad
+
     edge_trades = []
     for c in range(CHUNKS):
         r = pl.ds(c * rows, rows)
@@ -394,6 +394,15 @@
     if scatter:
         next_hop(3, 0)
         next_hop(2, 0)
+    for c in range(CHUNKS):
+        r = pl.ds(c * rows, rows)
+        edge_trades[c].wait_recv()
+        total = dmine[r].astype(F32) + dtheirs[r].astype(F32)
+        egrad_ref[r] = (live[r] * (ecot_ref[r].astype(F32) + total)).astype(BF)
+    stores = [load(12, egrad_ref, egrad_hbm)]
+    if scatter:
+        next_hop(3, 1)
+        next_hop(2, 1)
     for copy in backs:
         copy.wait_recv()
     fmine[...] = node_own + nn(lists, back_in[...].astype(BF))
@@ -401,25 +410,15 @@
     final = remote(fmine, ftheirs, mp_s.at[last], mp_r.at[last], other)
     final.start()
     if scatter:
-        next_hop(3, 1)
-        next_hop(2, 1)
-    for c in range(CHUNKS):
-        r = pl.ds(c * rows, rows)
-        edge_trades[c].wait_recv()
-        total = dmine[r].astype(F32) + dtheirs[r].astype(F32)
-        egrad_ref[r] = (live[r] * (ecot_ref[r].astype(F32) + total)).astype(BF)
-    if scatter:
         next_hop(3, 2)
         next_hop(2, 2)
-    stores = [load(12, egrad_ref, egrad_hbm)]
-    final.wait_recv()
-    ngrad_ref[...] = (ncot_ref[...].astype(F32) + fmine[...] + ftheirs[...]).astype(BF)
-    stores.append(load(11, ngrad_ref, ngrad_hbm))
-    if scatter:
         finish(1, nw2_out)
         finish(0, nw1_out)
     stores.append(load(15, nw1_out, nw1_grad_hbm))
     stores.append(load(16, nw2_out, nw2_grad_hbm))
+    final.wait_recv()
+    ngrad_ref[...] = (ncot_ref[...].astype(F32) + fmine[...] + ftheirs[...]).astype(BF)
+    stores.append(load(11, ngrad_ref, ngrad_hbm))
     if scatter:
         finish(3, ew2_out)
         finish(2, ew1_out)

time: 46.6 us -> 46.7 us (level)
  no operation moved by 1% of the time
where the time goes in v4:
time: 46.7 us; the launch traced here: 46.5 us
  Pallas kernels  45.2 us (97%)
  between operations  1.29 us (3%)
    pallas_call x1, Pallas kernels, local(): pl.pallas_call(functools.partial(kernel, (count, neigh, slots, scatter)),...  43 us
    pallas_call x1, Pallas kernels, write_out(): pl.pallas_call(write_kernel, out_shape=[jax.ShapeDtypeStruct(v.shape, v.d...  2.16 us

profile of v4, /device:TPU:0, one launch (start us, length us, event | category | flops | bytes accessed | tf_op | source)
XLA Modules:
  0.0 46.5 jit_solution(13608400383678062999)
XLA Ops:
  1.3 43.0 %shard_map.163 = (bf16[96,512]{1,0:T(8,128)(2,1)}, bf16[576,512]{1,0:T(8,128)(2,1)}, f32[192,256]{1,0:T(8,128)}, f32[64,256]{1,0:T(8,128)}, f32[128,256]{1,0:T(8,128)}, /*index=5*/f32[64,256]{1,0:T(8,128)}) custom-call(bf16[96,512]{1,0:T(8,128)(2,1)} %node_hbm.1, bf16[576,512]{1,0:T(8,128)(2,1)} %edge_hbm.1, bf16[96,512]{1,0:T(8,128)(2,1)} %ncot_hbm.1, ...), custom_call_target="tpu_custom_call" | custom-call | tf_op jit(solution)/shard_map/pallas_call | solution.py:566
  44.3 2.2 %shard_map.164 = (bf16[96,512]{1,0:T(8,128)(2,1)}, bf16[576,512]{1,0:T(8,128)(2,1)}, f32[192,256]{1,0:T(8,128)}, f32[64,256]{1,0:T(8,128)}, f32[128,256]{1,0:T(8,128)}, /*index=5*/f32[64,256]{1,0:T(8,128)}) custom-call(bf16[96,512]{1,0:T(8,128)(2,1)} %get-tuple-element.18.refs_0_, bf16[576,512]{1,0:T(8,128)(2,1)} %get-tuple-element.19.refs_1_, ...), custom_call_target="tpu_custom_call" | custom-call | tf_op jit(solution)/shard_map/pallas_call | solution.py:454
